TPU v7x, 128 devices: a whole 4x4x4 slice. The times are simulated.
128 devices in a mesh: wide: 32 (over z, y, x_lo), narrow: 4 (over x_hi, core).
Axes of the slice: x: 4 (x_hi: 2, x_lo: 2; x = x_hi * 2 + x_lo), y: 4, z: 4, core: 2. Of those that a mesh axis runs over, the one named last changes fastest.
Arguments:
- embedded: bfloat16 [16384, 4096], P('wide'), may hold values from -6 to 6
- cotangent: bfloat16 [16384, 4096], P('wide', 'narrow'), may hold values from -3 to 3
- cross_weight: bfloat16 [4096, 4096], P(None, 'narrow'), may hold values from -0.09375 to 0.09375
- cross_bias: float32 [4096], P('narrow'), may hold values from -6 to 6
- bag_size: int32 [16384, 32], P('wide'), may hold values from 1 to 2
- row_owner: int32 [4, 16384, 16, 1], P('narrow', 'wide'), may hold values from 0 to 31; in each aligned block of 8192 rows (0 to 8191, 8192 to 16383, ..., all dimensions but the last counted through in order) at most 512 rows name the same one
- row_id: int32 [4, 16384, 16], P('narrow', 'wide'), may hold values from 0 to 2047
- emb_table: float32 [65536, 128], P('wide'), may hold values from -6 to 6
- adagrad_state: float32 [65536], P('wide'), may hold values from 0.1 to 4
Outputs:
- weight_grad: float32 [4096, 4096], P('wide', 'narrow')
- bias_grad: float32 [4096], P('narrow')
- new_table: float32 [65536, 128], P('wide')
- new_state: float32 [65536], P('wide')
Inputs may be any that keep to these rules, and one draw needn't show every extreme that they name: `row_owner`: within the entries of one device (one index n of the first dimension and 512 aligned samples), no owner is named more than 512 times, a bound that some block reaches.
All inputs are finite; a program needn't handle non-finite values.
Results may differ from a plain program's by a relative error of at most 0.007.
Values may be sent and summed in bfloat16 or wider, within the bound.
No kernel may reach another device: no remote copies, remote signals or barrier semaphores. Data moves between devices by JAX's collectives and lax.ppermute only.
A program may use at most 128 MiB of HBM per device.

v0:
```python
import math

import jax
import jax.numpy as jnp
from jax import lax
from jax.sharding import PartitionSpec as P

LEARN_RATE = 0.3


def column_term(embedded, scaled_cols):
    return lax.dot_general(
        embedded, scaled_cols, (((0,), (0,)), ((), ())), preferred_element_type=jnp.float32
    )


def adagrad(grad_rows, table_rows, state_rows):
    state_next = state_rows + jnp.mean(grad_rows * grad_rows, axis=1)
    table_next = table_rows - LEARN_RATE * grad_rows / jnp.sqrt(state_next)[:, None]
    return (table_next, state_next)


def slot_positions(target, n_wide):
    entries = target.shape[0]
    block_len = math.gcd(entries, 512)
    block_count = entries // block_len
    onehot = (target[:, None] == jnp.arange(n_wide, dtype=jnp.int32)[None, :]).astype(jnp.bfloat16)
    blocked = onehot.reshape(block_count, block_len, n_wide)
    lower = (jnp.arange(block_len)[:, None] > jnp.arange(block_len)[None, :]).astype(jnp.bfloat16)
    within = jnp.einsum("ij,bjn->bin", lower, blocked, preferred_element_type=jnp.float32)
    block_total = jnp.sum(blocked.astype(jnp.float32), axis=1)
    before = jnp.cumsum(block_total, axis=0) - block_total
    counted = (within + before[:, None, :]) * blocked.astype(jnp.float32)
    return jnp.sum(counted, axis=2).reshape(entries).astype(jnp.int32)


def owned_sums(recv_values, recv_rows, owned_count):
    total_slots = recv_rows.shape[0]
    block_len = math.gcd(total_slots, 2048)
    block_count = total_slots // block_len
    value_blocks = recv_values.reshape(block_count, block_len, recv_values.shape[1])
    row_blocks = recv_rows.reshape(block_count, block_len)
    row_numbers = jnp.arange(owned_count, dtype=jnp.int32)

    def add_block(total, pair):
        rows_blk, values_blk = pair
        selector = (row_numbers[:, None] == rows_blk[None, :]).astype(jnp.bfloat16)
        return (total + jnp.dot(selector, values_blk, preferred_element_type=jnp.float32), None)

    start = jnp.zeros((owned_count, recv_values.shape[1]), jnp.float32)
    result, unused = lax.scan(add_block, start, (row_blocks, value_blocks))
    return result


def body(
    embedded,
    cotangent,
    cross_weight,
    cross_bias,
    bag_size,
    row_owner,
    row_id,
    emb_table,
    adagrad_state,
):
    panel_idx = lax.axis_index("narrow")
    panel_width = cross_weight.shape[1]
    batch_rows = embedded.shape[0]
    n_wide = lax.axis_size("wide")
    norm_factor = 1.0 / math.sqrt(batch_rows * n_wide)
    x_panel = lax.dynamic_slice_in_dim(embedded, panel_idx * panel_width, panel_width, 1)
    grad_out = cotangent.astype(jnp.float32)
    scaled = (grad_out * x_panel.astype(jnp.float32)).astype(jnp.bfloat16)
    cross_out = jnp.dot(embedded, cross_weight, preferred_element_type=jnp.float32) + cross_bias
    backward = lax.dot_general(
        scaled, cross_weight, (((1,), (1,)), ((), ())), preferred_element_type=jnp.float32
    )
    backward = lax.psum_scatter(backward, "narrow", scatter_dimension=1, tiled=True)
    pooled = (grad_out + backward + grad_out * cross_out).astype(jnp.bfloat16)
    emb_width = emb_table.shape[1]
    feats = panel_width // emb_width
    bag_depth = row_id.shape[2] // feats
    feature_grads = pooled.reshape(batch_rows, feats, 1, emb_width)
    bag_len = lax.dynamic_slice_in_dim(bag_size, panel_idx * feats, feats, 1)
    is_live = jnp.arange(bag_depth, dtype=jnp.int32)[None, None, :] < bag_len[:, :, None]
    values = jnp.where(is_live[:, :, :, None], feature_grads, jnp.zeros((), jnp.bfloat16)).reshape(
        -1, emb_width
    )
    target = row_owner.reshape(-1)
    local_row = row_id.reshape(-1)
    entries = target.shape[0]
    capacity = 2 * entries // n_wide
    position = slot_positions(target, n_wide)
    slots = target * capacity + position
    source = (
        jnp.full((n_wide * capacity,), entries, jnp.int32)
        .at[slots]
        .set(jnp.arange(entries, dtype=jnp.int32))
    )
    padded_values = jnp.concatenate([values, jnp.zeros((1, emb_width), jnp.bfloat16)], axis=0)
    padded_rows = jnp.concatenate([local_row, jnp.zeros((1,), jnp.int32)], axis=0)
    send_values = jnp.take(padded_values, source, axis=0).reshape(n_wide, capacity, emb_width)
    send_rows = jnp.take(padded_rows, source, axis=0).reshape(n_wide, capacity)
    recv_values, recv_rows = (
        lax.all_to_all(send_values, "wide", split_axis=0, concat_axis=0, tiled=True),
        lax.all_to_all(send_rows, "wide", split_axis=0, concat_axis=0, tiled=True),
    )
    partial_rows = owned_sums(
        recv_values.reshape(-1, emb_width), recv_rows.reshape(-1), emb_table.shape[0]
    )
    total_rows = lax.psum(partial_rows, "narrow")
    new_table, new_state = adagrad(total_rows, emb_table, adagrad_state)
    weight_grad = (
        lax.psum_scatter(column_term(embedded, scaled), "wide", scatter_dimension=0, tiled=True)
        * norm_factor
    )
    bias_grad = lax.psum(jnp.sum(scaled, axis=0, dtype=jnp.float32), "wide") * norm_factor
    return (weight_grad, bias_grad, new_table, new_state)


def solution(mesh):
    in_specs = (
        P("wide", None),
        P("wide", "narrow"),
        P(None, "narrow"),
        P("narrow"),
        P("wide", None),
        P("narrow", "wide", None, None),
        P("narrow", "wide", None),
        P("wide", None),
        P("wide"),
    )
    out_specs = (P("wide", "narrow"), P("narrow"), P("wide", None), P("wide"))
    return jax.shard_map(body, mesh=mesh, in_specs=in_specs, out_specs=out_specs, check_vma=False)
```

profile of v0, /device:TPU:24, one launch (start us, length us, event | category | flops | bytes accessed | tf_op | source)
XLA Modules:
  0.0 729.0 jit_solution(12705625604287005003)
XLA Ops:
  8.1 2.0 convert_reduce_fusion
  10.1 10.2 %fusion.24 = f32[512,4096]{1,0:T(8,128)} fusion(bf16[512,1024]{1,0:T(8,128)(2,1)S(1)} %get-tuple-element.74, bf16[4096,1024]{1,0:T(8,128)(2,1)} %param.13), kind=kOutput, calls=%fused_computation.51 | convolution fusion | flops 4294967296 | bytes 17825792 | tf_op jit(solution)/shard_map/dot_general | solution.py:75
  20.3 0.7 copy-done.6
  21.0 0.1 copy.22
  21.2 0.1 reshape.128
  21.3 0.1 copy.21
  21.5 0.1 copy.20
  21.6 0.2 mul.60
  21.8 0.2 eq.32
  21.9 0.2 convert_reduce_fusion.1
  22.2 0.6 fusion.14
  22.9 30.5 %scatter_custom_fusion = s32[16384]{0:T(1024)S(1)} fusion(s32[8192]{0:T(1024)S(1)} %bitcast.51, s32[8192]{0:T(1024)S(1)} %iota.32, s32[]{:T(128)} %constant.34.clone.1), kind=kCustom, calls=%fused_computation.44 | custom fusion | bytes 65540 | tf_op jit(solution)/shard_map/scatter | solution.py:98
  53.4 90.5 %gather_fusion = s32[16384]{0:T(1024)S(1)} fusion(s32[8193]{0:T(1024)S(1)} %pad_add_fusion, s32[16384]{0:T(1024)S(1)} %fusion.19), kind=kCustom, calls=%fused_computation | custom fusion | bytes 196608 | tf_op jit(solution)/shard_map/jit(_take)/gather | solution.py:103
  144.0 0.7 broadcast_select_fusion.2
  144.6 9.3 %all-to-all-start = ((s32[32,1,512]{2,1,0:T(1,128)}), s32[32,1,512]{2,1,0:T(1,128)S(1)}, u32[]{:S(2)}, u32[]{:S(2)}) async-start(s32[32,1,512]{2,1,0:T(1,128)} %bitcast.4), calls=%async_computation.1 | async-start | bytes 131072 | tf_op jit(solution)/shard_map/all_to_all | solution.py:106
  153.9 0.1 copy.23
  154.1 1.3 iota_compare_fusion.4
  155.4 1.6 lt.63
  157.1 9.8 %fusion.11 = bf16[64,8,8,128]{3,1,2,0:T(8,128)(2,1)S(1)} fusion(bf16[512,4096]{1,0:T(8,128)(2,1)} %param.11, bf16[4096,1024]{1,0:T(8,128)(2,1)} %param.13, f32[512,1024]{1,0:T(8,128)} %reduce-scatter.5.cloned.1.call-done, bf16[512,1024]{1,0:T(8,128)(2,1)S(1)} %copy-done.4, f32[1024]{0:T(1024)S(1)} %copy-done.8), kind=kOutput, calls=%fused_computation.23 | convolution fusion | flops 4298113024 | bytes 16781312 | tf_op jit(solution)/shard_map/dot_general | solution.py:74
  166.9 0.3 copy.26
  167.2 1.4 broadcast_in_dim.71
  168.6 4.3 broadcast_select_fusion.1
  172.9 0.2 concatenate.7
  173.1 57.4 %gather_fusion.1 = bf16[16384,128]{1,0:T(8,128)(2,1)} fusion(bf16[8193,128]{1,0:T(8,128)(2,1)S(1)} %concatenate.7, s32[16384]{0:T(1024)S(1)} %fusion.19), kind=kCustom, calls=%fused_computation.1 | custom fusion | bytes 8454144 | tf_op jit(solution)/shard_map/jit(_take)/gather | solution.py:102
  230.5 7.6 %broadcast_select_fusion = bf16[32,512,128]{2,1,0:T(8,128)(2,1)} fusion(bf16[32,512,128]{2,1,0:T(8,128)(2,1)} %bitcast.46, pred[32,512]{1,0:T(8,128)(4,1)S(1)} %broadcast_in_dim.67), kind=kLoop, calls=%fused_computation.13 | loop fusion | flops 2097152 | bytes 8404992 | tf_op jit(solution)/shard_map/jit(_take)/select_n | solution.py:102
  238.1 8.4 %all-to-all-start.1 = ((bf16[32,512,128]{2,1,0:T(8,128)(2,1)}), bf16[32,512,128]{2,1,0:T(8,128)(2,1)}, u32[]{:S(2)}, u32[]{:S(2)}) async-start(bf16[32,512,128]{2,1,0:T(8,128)(2,1)} %broadcast_select_fusion), calls=%async_computation.3 | async-start | bytes 8388608 | tf_op jit(solution)/shard_map/all_to_all | solution.py:105
  246.5 0.3 all-reduce.3.cloned.1.call-start
  246.7 0.2 reduce
  247.0 49.3 %all-to-all-done.1 = bf16[32,512,128]{2,1,0:T(8,128)(2,1)} async-done(((bf16[32,512,128]{2,1,0:T(8,128)(2,1)}), bf16[32,512,128]{2,1,0:T(8,128)(2,1)}, u32[]{:S(2)}, u32[]{:S(2)}) %all-to-all-start.1) | async-done | bytes 4194336 | tf_op jit(solution)/shard_map/all_to_all | solution.py:105
  296.3 35.2 %while.11 = (s32[]{:T(128)}, f32[2048,128]{1,0:T(8,128)S(1)}, s32[8,2048]{1,0:T(8,128)S(1)}, bf16[8,2048,128]{2,1,0:T(8,128)(2,1)}, s32[]{:T(128)}, /*index=5*/s32[]{:T(128)}) while((s32[]{:T(128)}, f32[2048,128]{1,0:T(8,128)S(1)}, s32[8,2048]{1,0:T(8,128)S(1)}, bf16[8,2048,128]{2,1,0:T(8,128)(2,1)}, s32[]{:T(128)}, ...), condition=%wide.region_9.10_spmd.clone, body=%wide.region_8.9_spmd.clone.sunk | while | flops 1078460416 | bytes 2646111 | solution.py:51
  296.3 4.4 fusion.34
  300.7 4.4 fusion.34
  305.1 4.4 fusion.34
  309.5 4.4 fusion.34
  313.9 4.4 fusion.34
  318.3 4.4 fusion.34
  322.7 4.4 fusion.34
  327.1 4.4 fusion.34
  331.5 1.0 copy-done.3
  332.5 10.3 %convolution_bitcast_fusion = f32[4096,1024]{0,1:T(8,128)} fusion(bf16[512,1024]{1,0:T(8,128)(2,1)S(1)} %get-tuple-element.74, bf16[512,4096]{1,0:T(8,128)(2,1)} %param.11), kind=kOutput, calls=%fused_computation.12 | convolution fusion | flops 4294967296 | bytes 22020096 | tf_op jit(solution)/shard_map/dot_general | solution.py:12
  342.9 77.2 %psum.14 = f32[1024]{0:T(1024)S(1)} all-reduce(f32[1024]{0:T(1024)S(1)} %get-tuple-element.73), channel_id=1, replica_groups=mesh['wide'=32,'narrow'=4] {'wide'}, use_global_device_ids=true, to_apply=%region_2.3 | all-reduce | flops 1024 | bytes 8192 | tf_op jit(solution)/shard_map/psum | solution.py:117
  420.1 0.6 broadcast_multiply_fusion.2
  420.7 1.6 multiply_reduce_fusion
  422.3 0.6 fusion.22
  422.9 2.5 divide_subtract_fusion
  425.5 294.0 %reduce-scatter.3.cloned.1.call-done = f32[128,1024]{0,1:T(8,128)} async-done(((f32[4096,1024]{0,1:T(8,128)}), f32[128,1024]{0,1:T(8,128)}) %reduce-scatter.3.cloned.1.call-update) | async-done | bytes 524304 | tf_op jit(solution)/shard_map/reduce_scatter | solution.py:114
  719.5 1.1 broadcast_multiply_fusion
  720.5 1.0 copy.24
  (45 shorter events, 0.6 us)
Async XLA Ops:
  8.0 145.9 %copy-start = (s32[512,32]{0,1:T(8,128)S(1)}, s32[512,32]{0,1:T(8,128)}, u32[]{:S(2)}) copy-start(s32[512,32]{0,1:T(8,128)} %param.15) | copy-start | bytes 196612
  8.0 149.0 %reduce-scatter.5.cloned.1.call-start = ((), (), s32[]{:S(2)}) async-start(), calls=%async_computation.5 | async-start | bytes 10485760 | tf_op jit(solution)/shard_map/reduce_scatter | solution.py:78
  20.3 0.8 copy-start.6
  20.3 1.0 copy-start.5
  53.4 103.6 %copy-start.4 = (bf16[512,1024]{1,0:T(8,128)(2,1)S(1)}, bf16[512,1024]{1,0:T(8,128)(2,1)}, u32[]{:S(2)}) copy-start(bf16[512,1024]{1,0:T(8,128)(2,1)} %param.12) | copy-start | bytes 3145732
  53.4 103.6 %copy-start.8 = (f32[1024]{0:T(1024)S(1)}, f32[1024]{0:T(1024)}, u32[]{:S(2)}) copy-start(f32[1024]{0:T(1024)} %param.14) | copy-start | bytes 12292
  144.6 93.5 %all-to-all-start = ((s32[32,1,512]{2,1,0:T(1,128)}), s32[32,1,512]{2,1,0:T(1,128)S(1)}, u32[]{:S(2)}, u32[]{:S(2)}) async-start(s32[32,1,512]{2,1,0:T(1,128)} %bitcast.4), calls=%async_computation.1 | async-start | bytes 131072 | tf_op jit(solution)/shard_map/all_to_all | solution.py:106
  238.1 58.2 %all-to-all-start.1 = ((bf16[32,512,128]{2,1,0:T(8,128)(2,1)}), bf16[32,512,128]{2,1,0:T(8,128)(2,1)}, u32[]{:S(2)}, u32[]{:S(2)}) async-start(bf16[32,512,128]{2,1,0:T(8,128)(2,1)} %broadcast_select_fusion), calls=%async_computation.3 | async-start | bytes 8388608 | tf_op jit(solution)/shard_map/all_to_all | solution.py:105
  246.5 174.3 %all-reduce.3.cloned.1.call-start = ((), (), s32[]{:S(2)}) async-start(), calls=%async_computation.6 | async-start | bytes 2097152 | tf_op jit(solution)/shard_map/psum | solution.py:111
  331.5 1.0 copy-start.3
  332.5 387.0 %reduce-scatter.3.cloned.1.call-start = ((), (), s32[]{:S(2)}) async-start(), calls=%async_computation.4 | async-start | bytes 17301504 | tf_op jit(solution)/shard_map/reduce_scatter | solution.py:114
  342.9 79.4 %copy-start.7 = (f32[2048]{0:T(1024)S(1)}, f32[2048]{0:T(1024)}, u32[]{:S(2)}) copy-start(f32[2048]{0:T(1024)} %param.19) | copy-start | bytes 24580
  342.9 80.0 %copy-start.2 = (f32[2048,128]{1,0:T(8,128)S(1)}, f32[2048,128]{1,0:T(8,128)}, u32[]{:S(2)}) copy-start(f32[2048,128]{1,0:T(8,128)} %param.18) | copy-start | bytes 3145732
  342.9 378.6 %copy-start.1 = (s32[512,32]{0,1:T(8,128)S(1)}, s32[512,32]{0,1:T(8,128)}, u32[]{:S(2)}) copy-start(s32[512,32]{0,1:T(8,128)} %param.15) | copy-start | bytes 196612
Sparse Core Ops, SparseCore 0:
  20.4 80.6 reduce-scatter.4
  332.6 81.1 all-reduce.2
Sparse Core Ops, SparseCore 1:
  343.0 376.4 reduce-scatter.2
where the time goes:
time: 735 us; the launch traced here: 729 us
  waiting for transfers between devices  343 us (47%)
  local copies, waits for them, and re-layouts  186 us (25%)
  blocking collectives  77.2 us (11%)
  matrix products  65.8 us (9%)
  other arithmetic  22.7 us (3%)
  starting transfers between devices  18 us (2%)
  between operations  15.8 us (2%)
    reduce_scatter x1, waiting for transfers between devices, body(): lax.psum_scatter(column_term(embedded, scaled), 'wide', scatter_dimension...  294 us
    gather x1, local copies, waits for them, and re-layouts, body(): send_rows = jnp.take(padded_rows, source, axis=0).reshape(n_wide, capacity)  90.5 us
    psum x1, blocking collectives, body(): lax.psum(jnp.sum(scaled, axis=0, dtype=jnp.float32), 'wide') * norm_factor  77.2 us
    gather x1, local copies, waits for them, and re-layouts, body(): jnp.take(padded_values, source, axis=0).reshape(n_wide, capacity, emb_width)  57.4 us
    all_to_all x1, waiting for transfers between devices, body(): lax.all_to_all(send_values, 'wide', split_axis=0, concat_axis=0, tiled=True)  49.3 us
    dot_general x8, matrix products, add_block(): jnp.dot(selector, values_blk, preferred_element_type=jnp.float32)  34.9 us
    scatter x1, local copies, waits for them, and re-layouts, body(): source = jnp.full((n_wide * capacity,), entries, jnp.int32).at[slots].set...  30.5 us
  transfers between devices with their start and end apart: 5, of which 2 were waited for; matrix products, arithmetic and copies ran while one was open for 31% of the time, Pallas kernels for 0%

commit v1 on v0

v1 whole, which is shorter than its diff:
```python
import math

import jax
import jax.numpy as jnp
from jax import lax
from jax.experimental import pallas as pl
from jax.experimental.pallas import tpu as pltpu
from jax.sharding import PartitionSpec as P

LEARN_RATE = 0.3
E = 128
N_WIDE = 32
CAP = 512
ID_ROWS = 16
BLOCK = CAP + ID_ROWS
N_ROWS = 2048
HI = 4
LO = N_ROWS // HI
F32 = jnp.float32
BF16 = jnp.bfloat16


def z_perm(d):
    return [(i, ((i // 8 + d) % 4) * 8 + i % 8) for i in range(N_WIDE)]


def y_perm(d):
    return [(i, (i // 8) * 8 + (((i // 2) % 4 + d) % 4) * 2 + i % 2) for i in range(N_WIDE)]


X_LO = [(i, i ^ 1) for i in range(N_WIDE)]
CORE = [(i, i ^ 1) for i in range(4)]
X_HI = [(i, i ^ 2) for i in range(4)]


def slot_positions(onehot):
    entries, n_wide = onehot.shape
    block_len = 512
    block_count = entries // block_len
    blocked = onehot.reshape(block_count, block_len, n_wide)
    lower = (jnp.arange(block_len)[:, None] > jnp.arange(block_len)[None, :]).astype(BF16)
    within = jnp.einsum("ij,bjn->bin", lower, blocked, preferred_element_type=F32)
    block_total = jnp.sum(blocked.astype(F32), axis=1)
    before = jnp.cumsum(block_total, axis=0) - block_total
    counted = (within + before[:, None, :]) * blocked.astype(F32)
    position = jnp.sum(counted, axis=2).reshape(entries).astype(jnp.int32)
    return position, jnp.sum(block_total, axis=0)


def scatter_kernel(slots_ref, base_ref, far_ref, ids_ref, out_ref, rows):
    dump = N_WIDE * CAP

    def clear(i, _):
        rows[pl.ds(pl.multiple_of(i * 64, 64), 64), :] = jnp.zeros((64, E), F32)
        return 0

    lax.fori_loop(0, dump // 64, clear, 0)

    def place(i, _):
        first = pl.multiple_of(i * 16, 16)
        for f in range(8):
            cols = slice(f * E, (f + 1) * E)
            tile = base_ref[pl.ds(first, 16), cols] + far_ref[pl.ds(first, 16), cols].astype(F32)
            for b in range(16):
                row = tile[b : b + 1, :]
                for j in range(2):
                    slot = slots_ref[(first + b) * 16 + 2 * f + j]
                    rows[pl.ds(slot, 1), :] = row
        return 0

    lax.fori_loop(0, base_ref.shape[0] // 16, place, 0)

    def narrow_down(w, _):
        out_ref[w, :CAP, :] = rows[pl.ds(pl.multiple_of(w * CAP, CAP), CAP), :].astype(BF16)
        out_ref[w, CAP:, :] = ids_ref[w]
        return 0

    lax.fori_loop(0, N_WIDE, narrow_down, 0)


def scatter_entries(slots, base, far, ids):
    vmem = pl.BlockSpec(memory_space=pltpu.VMEM)
    return pl.pallas_call(
        scatter_kernel,
        out_shape=jax.ShapeDtypeStruct((N_WIDE, BLOCK, E), BF16),
        in_specs=[pl.BlockSpec(memory_space=pltpu.SMEM), vmem, vmem, vmem],
        out_specs=vmem,
        scratch_shapes=[pltpu.VMEM((N_WIDE * CAP + 8, E), F32)],
        compiler_params=pltpu.CompilerParams(vmem_limit_bytes=40 << 20),
        cost_estimate=pl.CostEstimate(flops=0, bytes_accessed=40 << 20, transcendentals=0),
        name="place_entries",
    )(slots, base, far, ids)


def sums_kernel(count_ref, recv_ref, out_ref, total):
    total[...] = jnp.zeros_like(total)
    lane_rows = lax.broadcasted_iota(jnp.int32, (LO, E), 0)

    def add_half(w, half):
        ids = recv_ref[w, CAP:, :].astype(F32)
        row = (ids[0:4, :] * 64.0 + ids[4:8, :]).astype(jnp.int32) - 1
        hi = row // LO
        lo = row - hi * LO
        hi = jnp.where(row < 0, -1, hi)
        hi_col = jnp.transpose(jnp.concatenate([hi, hi], axis=0).astype(F32), (1, 0))
        left, right = [], []
        for j in range(half * 2, half * 2 + 2):
            left.append(jnp.where(lane_rows == lo[j : j + 1, :], 1.0, 0.0).astype(BF16))
            v = recv_ref[w, j * E : (j + 1) * E, :]
            own = jnp.broadcast_to(hi_col[:, j : j + 1], (E, E)).astype(BF16)
            right.append(
                jnp.concatenate(
                    [jnp.where(own == BF16(h), v, BF16(0)) for h in range(HI)], axis=1
                )
            )
        total[...] += jnp.dot(
            jnp.concatenate(left, axis=1),
            jnp.concatenate(right, axis=0),
            preferred_element_type=F32,
        )

    def source(w, _):
        count = count_ref[w]
        for half in range(2):

            @pl.when(count > half * 2 * E)
            def _():
                add_half(w, half)

        return 0

    lax.fori_loop(0, N_WIDE, source, 0)
    for h in range(HI):
        out_ref[h * LO : (h + 1) * LO, :] = total[:, h * E : (h + 1) * E].astype(BF16)


def owned_sums(counts, recv):
    vmem = pl.BlockSpec(memory_space=pltpu.VMEM)
    return pl.pallas_call(
        sums_kernel,
        out_shape=jax.ShapeDtypeStruct((N_ROWS, E), BF16),
        in_specs=[pl.BlockSpec(memory_space=pltpu.SMEM), vmem],
        out_specs=vmem,
        scratch_shapes=[pltpu.VMEM((LO, HI * E), F32)],
        compiler_params=pltpu.CompilerParams(vmem_limit_bytes=40 << 20),
        cost_estimate=pl.CostEstimate(flops=8 << 30, bytes_accessed=5 << 20, transcendentals=0),
        name="owned_sums",
    )(counts, recv)


def summed(own, others):
    total = own.astype(F32)
    for other in others:
        total = total + other.astype(F32)
    return total


def weight_grad_owned(embedded, scaled, z, y, x_lo):
    half = scaled.shape[1] // 2
    left, right = scaled[:, :half], scaled[:, half:]
    dims = (((0,), (0,)), ((), ()))

    def term_z(d):
        rows = lax.dynamic_slice_in_dim(embedded, ((z + d) % 4) * 1024, 1024, 1)
        return lax.dot_general(rows, left, dims, preferred_element_type=F32).astype(BF16)

    def term_y(d):
        start = ((y + d) % 4) * 256
        rows = jnp.concatenate(
            [lax.dynamic_slice_in_dim(embedded, k * 1024 + start, 256, 1) for k in range(4)], axis=1
        )
        return lax.dot_general(rows, right, dims, preferred_element_type=F32).astype(BF16)

    got_z = [lax.ppermute(term_z(d), "wide", z_perm(d)) for d in (2, 1, 3)]
    got_y = [lax.ppermute(term_y(d), "wide", y_perm(d)) for d in (2, 1, 3)]
    by_z = summed(term_z(0), got_z).astype(BF16)
    by_y = summed(term_y(0), got_y).astype(BF16)

    def piece(array, at):
        return lax.dynamic_slice_in_dim(array, (at % 4) * 256, 256, 0)

    got_zy = [lax.ppermute(piece(by_z, y + d), "wide", y_perm(d)) for d in (2, 1, 3)]
    got_yz = [lax.ppermute(piece(by_y, z + d), "wide", z_perm(d)) for d in (2, 1, 3)]
    pair = jnp.concatenate(
        [summed(piece(by_z, y), got_zy), summed(piece(by_y, z), got_yz)], axis=1
    ).astype(BF16)
    got = lax.ppermute(lax.dynamic_slice_in_dim(pair, (1 - x_lo) * E, E, 0), "wide", X_LO)
    return summed(lax.dynamic_slice_in_dim(pair, x_lo * E, E, 0), [got])


def over_narrow(part, core):
    rows = part.shape[0] // 2
    keep = lax.dynamic_slice_in_dim(part, core * rows, rows, 0)
    send = lax.dynamic_slice_in_dim(part, (1 - core) * rows, rows, 0)
    chip = summed(keep, [lax.ppermute(send, "narrow", CORE)]).astype(BF16)
    mine = summed(chip, [lax.ppermute(chip, "narrow", X_HI)])
    mate = lax.ppermute(mine, "narrow", CORE)
    low = jnp.where(core == 0, mine, mate)
    high = jnp.where(core == 0, mate, mine)
    return jnp.concatenate([low, high], axis=0)


def body(
    embedded,
    cotangent,
    cross_weight,
    cross_bias,
    bag_size,
    row_owner,
    row_id,
    emb_table,
    adagrad_state,
):
    panel = lax.axis_index("narrow")
    wide = lax.axis_index("wide")
    z, y, x_lo = wide // 8, (wide // 2) % 4, wide % 2
    core = panel % 2
    batch_rows, width = cotangent.shape
    feats = width // E
    norm_factor = 1.0 / math.sqrt(batch_rows * N_WIDE)

    x_panel = lax.dynamic_slice_in_dim(embedded, panel * width, width, 1)
    grad_out = cotangent.astype(F32)
    scaled = (grad_out * x_panel.astype(F32)).astype(BF16)

    def backward_part(k):
        rows = lax.dynamic_slice_in_dim(cross_weight, (panel ^ k) * width, width, 0)
        return lax.dot_general(scaled, rows, (((1,), (1,)), ((), ())), preferred_element_type=F32)

    from_mate_far = lax.ppermute(backward_part(3).astype(BF16), "narrow", CORE)
    chip_far = (backward_part(2) + from_mate_far.astype(F32)).astype(BF16)
    far = lax.ppermute(chip_far, "narrow", X_HI)
    from_mate = lax.ppermute(backward_part(1).astype(BF16), "narrow", CORE)
    cross_out = jnp.dot(embedded, cross_weight, preferred_element_type=F32) + cross_bias
    base = grad_out + grad_out * cross_out + backward_part(0) + from_mate.astype(F32)

    bag_len = lax.dynamic_slice_in_dim(bag_size, panel * feats, feats, 1)
    bag_depth = row_id.shape[2] // feats
    is_live = (jnp.arange(bag_depth, dtype=jnp.int32)[None, None, :] < bag_len[:, :, None]).reshape(-1)
    target = jnp.where(is_live, row_owner.reshape(-1), N_WIDE)
    is_target = target[:, None] == jnp.arange(N_WIDE, dtype=jnp.int32)[None, :]
    onehot = is_target.astype(BF16)
    position, counts = slot_positions(onehot)
    slots = jnp.where(is_live, target * CAP + position, N_WIDE * CAP)
    marked = row_id.reshape(-1) + 1
    halves = jnp.concatenate(
        [
            jnp.where(is_target, (marked // 64)[:, None], 0),
            jnp.where(is_target, (marked % 64)[:, None], 0),
        ],
        axis=1,
    ).astype(BF16)
    at_position = (position[:, None] == jnp.arange(CAP, dtype=jnp.int32)[None, :]).astype(BF16)
    ids = lax.dot_general(halves, at_position, (((0,), (0,)), ((), ())), preferred_element_type=F32)
    ids = ids.astype(BF16).reshape(2, N_WIDE, CAP // E, E).transpose(1, 0, 2, 3)
    ids = jnp.pad(ids.reshape(N_WIDE, 2 * CAP // E, E), ((0, 0), (0, ID_ROWS - 2 * CAP // E), (0, 0)))

    bias_part = jnp.sum(scaled, axis=0, dtype=F32)
    shared = lax.all_gather(jnp.concatenate([bias_part, counts]), "wide")
    bias_grad = jnp.sum(shared[:, :width], axis=0) * norm_factor
    recv_counts = lax.dynamic_slice_in_dim(shared, width + wide, 1, 1).reshape(-1).astype(jnp.int32)

    payload = scatter_entries(slots, base, far, ids)
    recv = lax.all_to_all(payload, "wide", split_axis=0, concat_axis=0, tiled=True)
    row_grad = over_narrow(owned_sums(recv_counts, recv), core)
    new_state = adagrad_state + jnp.mean(row_grad * row_grad, axis=1)
    new_table = emb_table - LEARN_RATE * row_grad / jnp.sqrt(new_state)[:, None]

    weight_grad = weight_grad_owned(embedded, scaled, z, y, x_lo) * norm_factor
    return (weight_grad, bias_grad, new_table, new_state)


def solution(mesh):
    in_specs = (
        P("wide", None),
        P("wide", "narrow"),
        P(None, "narrow"),
        P("narrow"),
        P("wide", None),
        P("narrow", "wide", None, None),
        P("narrow", "wide", None),
        P("wide", None),
        P("wide"),
    )
    out_specs = (P("wide", "narrow"), P("narrow"), P("wide", None), P("wide"))
    return jax.shard_map(body, mesh=mesh, in_specs=in_specs, out_specs=out_specs, check_vma=False)
```

time: 735 us -> 538 us (0.73)
  local copies, waits for them, and re-layouts: 186 us -> 14.8 us
  blocking collectives: 77.2 us -> 0 us
  starting transfers between devices: 18 us -> 48.7 us
  Pallas kernels: 0 us -> 30.1 us
  waiting for transfers between devices: 343 us -> 369 us
  matrix products: 65.8 us -> 44.5 us
  other arithmetic: 22.7 us -> 9.86 us
    unnamed x3 -> x2, waiting for transfers between devices: 0.05 us -> 295 us
    reduce_scatter x2 -> x0, waiting for transfers between devices: 294 us -> none  [the longest x1 294 us: body(): lax.psum_scatter(column_term(embedded, scaled), 'wide', scatter_dimension...]
    gather x2 -> x0, local copies, waits for them, and re-layouts: 148 us -> none  [the longest x1 90.5 us: body(): send_rows = jnp.take(padded_rows, source, axis=0).reshape(n_wide, capacity)]
    psum x1 -> x0, blocking collectives: 77.2 us -> none  [body(): lax.psum(jnp.sum(scaled, axis=0, dtype=jnp.float32), 'wide') * norm_factor]
    ppermute x0 -> x19, waiting for transfers between devices: none -> 73.8 us  [the longest x3 45.1 us: weight_grad_owned(): got_z = [lax.ppermute(term_z(d), 'wide', z_perm(d)) for d in (2, 1, 3)]]
    all_to_all x2 -> x1, waiting for transfers between devices: 49.3 us -> 0.01 us  [body(): lax.all_to_all(payload, 'wide', split_axis=0, concat_axis=0, tiled=True)]
    ppermute x0 -> x19, starting transfers between devices: none -> 39.4 us  [the longest x3 13.9 us: weight_grad_owned(): lax.ppermute(piece(by_y, z + d), 'wide', z_perm(d))]
    scatter x1 -> x0, local copies, waits for them, and re-layouts: 30.5 us -> none  [body(): source = jnp.full((n_wide * capacity,), entries, jnp.int32).at[slots].set...]
  transfers between devices with their start and end apart: 5 -> 21, of which waited for: 2 -> 6; matrix products, arithmetic and copies ran while one was open for 31% -> 11% of each run, Pallas kernels for 0% -> 3%
where the time goes in v1:
time: 538 us; the launch traced here: 533 us
  waiting for transfers between devices  369 us (69%)
  starting transfers between devices  48.7 us (9%)
  matrix products  44.5 us (8%)
  Pallas kernels  30.1 us (6%)
  between operations  15.4 us (3%)
  local copies, waits for them, and re-layouts  14.8 us (3%)
  other arithmetic  9.86 us (2%)
    unnamed x2, waiting for transfers between devices  295 us
    ppermute x3, waiting for transfers between devices, weight_grad_owned(): got_z = [lax.ppermute(term_z(d), 'wide', z_perm(d)) for d in (2, 1, 3)]  45.1 us
    pallas_call x1, Pallas kernels, owned_sums(): pl.pallas_call(sums_kernel, out_shape=jax.ShapeDtypeStruct((N_ROWS, E), B...  17.7 us
    ppermute x1, waiting for transfers between devices, body(): far = lax.ppermute(chip_far, 'narrow', X_HI)  15.2 us
    ppermute x3, starting transfers between devices, weight_grad_owned(): lax.ppermute(piece(by_y, z + d), 'wide', z_perm(d))  13.9 us
    dot_general x4, matrix products, backward_part(): lax.dot_general(scaled, rows, (((1,), (1,)), ((), ())), preferred_element...  12.9 us
    pallas_call x1, Pallas kernels, scatter_entries(): pl.pallas_call(scatter_kernel, out_shape=jax.ShapeDtypeStruct((N_WIDE, BL...  12.4 us
    dot_general x4, matrix products, term_z(): lax.dot_general(rows, left, dims, preferred_element_type=F32).astype(BF16)  11.7 us
  transfers between devices with their start and end apart: 21, of which 6 were waited for; matrix products, arithmetic and copies ran while one was open for 11% of the time, Pallas kernels for 3%

profile of v1, /device:TPU:24, one launch (start us, length us, event | category | flops | bytes accessed | tf_op | source)
XLA Modules:
  0.0 532.7 jit_solution(17739025265787138416)
XLA Ops:
  7.2 2.0 convert_reduce_fusion
  9.2 2.9 fusion.13
  12.2 3.9 fusion.16
  16.7 1.3 iota_compare_fusion.2
  18.0 1.6 lt.241
  19.6 1.6 lt.244
  23.1 2.9 fusion.23
  26.1 2.9 fusion.11
  29.0 3.3 add_convert_fusion
  32.3 3.3 collective-permute-start.15
  35.7 8.4 %fusion.4.base_ref = f32[512,1024]{1,0:T(8,128)S(1)} fusion(f32[512,1024]{1,0:T(8,128)S(1)} %fusion.11, bf16[512,1024]{1,0:T(8,128)(2,1)S(1)} %copy-done.5, bf16[512,1024]{1,0:T(8,128)(2,1)} %collective-permute-done.13, bf16[512,4096]{1,0:T(8,128)(2,1)S(1)} %copy-done.3, bf16[4096,1024]{1,0:T(8,128)(2,1)} %param.11, f32[1024]{0:T(1024)S(1)} %copy-done.15), kind=kOutput, calls=%fused_computation.7 | convolution fusion | flops 4298637312 | bytes 18878464 | tf_op jit(solution)/shard_map/dot_general | solution.py:234
  44.0 15.2 %collective-permute-done.15.far_ref = bf16[512,1024]{1,0:T(8,128)(2,1)S(1)} collective-permute-done((bf16[512,1024]{1,0:T(8,128)(2,1)S(1)}, bf16[512,1024]{1,0:T(8,128)(2,1)S(1)}, u32[]{:S(2)}, u32[]{:S(2)}) %collective-permute-start.15) | collective-permute-done | bytes 1048608 | tf_op jit(solution)/shard_map/ppermute | solution.py:232
  59.2 12.4 %place_entries.1 = bf16[32,528,128]{2,1,0:T(8,128)(2,1)S(1)} custom-call(s32[8192]{0:T(1024)S(1)} %get-tuple-element.51.slots_ref, f32[512,1024]{1,0:T(8,128)S(1)} %fusion.4.base_ref, bf16[512,1024]{1,0:T(8,128)(2,1)S(1)} %collective-permute-done.15.far_ref, bf16[32,16,128]{2,1,0:T(8,128)(2,1)S(1)} %pad.4.ids_ref), custom_call_target="tpu_custom_call" | custom-call | bytes 41943040 | tf_op jit(solution)/shard_map/place_entries/pallas_call | solution.py:83
  71.6 2.1 copy-done.2
  73.7 9.3 %all-to-all-start = ((bf16[32,528,128]{2,1,0:T(8,128)(2,1)}), bf16[32,528,128]{2,1,0:T(8,128)(2,1)}, u32[]{:S(2)}, u32[]{:S(2)}) async-start(bf16[32,528,128]{2,1,0:T(8,128)(2,1)} %copy-done.2), calls=%async_computation | async-start | bytes 8650752 | tf_op jit(solution)/shard_map/all_to_all | solution.py:264
  83.1 2.9 convolution_convert_fusion.4
  86.0 2.8 collective-permute-start.2
  88.8 3.0 convolution_convert_fusion.5
  91.8 2.9 convolution_convert_fusion.6
  94.7 2.3 collective-permute-start
  97.0 3.4 constant_dynamic-slice_fusion.20
  100.4 1.7 convolution_convert_fusion
  102.1 0.8 collective-permute-start.8
  103.0 1.7 convolution_convert_fusion.1
  104.7 2.4 collective-permute-start.7
  107.1 1.7 convolution_convert_fusion.2
  108.9 45.1 %collective-permute-done.2 = bf16[1024,512]{0,1:T(8,128)(2,1)S(1)} collective-permute-done((bf16[1024,512]{0,1:T(8,128)(2,1)}, bf16[1024,512]{0,1:T(8,128)(2,1)S(1)}, u32[]{:S(2)}, u32[]{:S(2)}) %collective-permute-start.2) | collective-permute-done | bytes 1048608 | tf_op jit(solution)/shard_map/ppermute | solution.py:174
  153.9 2.5 collective-permute-start.6
  158.8 295.4 %all-reduce.4.cloned.1.call-done = f32[33792]{0:T(1024)} async-done(((f32[33792]{0:T(1024)}), f32[33792]{0:T(1024)}) %all-reduce.4.cloned.1.call-update) | async-done | bytes 135184
  454.3 1.0 reshape.120
  455.6 1.0 copy-done.14
  456.5 2.8 add_convert_fusion.2
  459.4 0.9 constant_dynamic-slice_fusion.23
  460.3 2.1 collective-permute-start.5
  462.3 3.9 collective-permute-start.4
  466.3 1.5 collective-permute-start.3
  467.8 2.8 add_convert_fusion.1
  470.6 17.7 %owned_sums.1 = bf16[2048,128]{1,0:T(8,128)(2,1)S(1)} custom-call(s32[32]{0:T(128)S(1)} %convert_reduce_fusion.3.count_ref, bf16[32,528,128]{2,1,0:T(8,128)(2,1)} %all-to-all-done.recv_ref), custom_call_target="tpu_custom_call" | custom-call | flops 8589934592 | bytes 5242880 | tf_op jit(solution)/shard_map/owned_sums/pallas_call | solution.py:139
  488.7 2.0 collective-permute-start.10
  490.7 11.8 %collective-permute-start.9 = (bf16[256,512]{0,1:T(8,128)(2,1)S(1)}, bf16[256,512]{0,1:T(8,128)(2,1)S(1)}, u32[]{:S(2)}, u32[]{:S(2)}) collective-permute-start(bf16[256,512]{0,1:T(8,128)(2,1)S(1)} %get-tuple-element.44), channel_id=1, source_target_pairs={{0,64},{4,68},{8,72},{12,76},{16,80},{20,84},{24,88},{28,92},{32,9... | collective-permute-start | bytes 786440 | tf_op jit(solution)/shard_map/ppermute | solution.py:183
  502.5 1.2 add_convert_fusion.5
  503.9 3.2 collective-permute-start.17
  507.0 0.7 collective-permute-done.10
  507.7 6.8 %collective-permute-done.9 = bf16[256,512]{0,1:T(8,128)(2,1)S(1)} collective-permute-done((bf16[256,512]{0,1:T(8,128)(2,1)S(1)}, bf16[256,512]{0,1:T(8,128)(2,1)S(1)}, u32[]{:S(2)}, u32[]{:S(2)}) %collective-permute-start.9) | collective-permute-done | bytes 262176 | tf_op jit(solution)/shard_map/ppermute | solution.py:183
  514.8 0.8 convert_add_fusion
  516.3 6.1 %collective-permute-done.12 = bf16[128,1024]{0,1:T(8,128)(2,1)S(1)} collective-permute-done((bf16[128,1024]{0,1:T(8,128)(2,1)S(1)}, bf16[128,1024]{0,1:T(8,128)(2,1)S(1)}, u32[]{:S(2)}, u32[]{:S(2)}) %collective-permute-start.12) | collective-permute-done | bytes 262176 | tf_op jit(solution)/shard_map/ppermute | solution.py:187
  522.5 1.0 copy.57
  524.6 1.3 divide_subtract_fusion
  (92 shorter events, 7.0 us)
Async XLA Ops:
  7.2 9.4 %copy-start = (s32[512,32]{0,1:T(8,128)S(1)}, s32[512,32]{0,1:T(8,128)}, u32[]{:S(2)}) copy-start(s32[512,32]{0,1:T(8,128)} %param.13) | copy-start | bytes 196612
  12.1 23.6 %collective-permute-start.13 = (bf16[512,1024]{1,0:T(8,128)(2,1)S(1)}, bf16[512,1024]{1,0:T(8,128)(2,1)}, u32[]{:S(2)}, u32[]{:S(2)}) collective-permute-start(bf16[512,1024]{1,0:T(8,128)(2,1)S(1)} %fusion.13), channel_id=1, source_target_pairs={{0,1},{1,0},{2,3},{3,2},{4,5},{5,4},{6,7},{7,6},{8,9},{9,8},{10,11... | collective-permute-start | bytes 3145736 | tf_op jit(solution)/shard_map/ppermute | solution.py:233
  16.1 5.1 copy-start.11
  16.1 13.0 %collective-permute-start.14 = (bf16[512,1024]{1,0:T(8,128)(2,1)}, bf16[512,1024]{1,0:T(8,128)(2,1)}, u32[]{:S(2)}, u32[]{:S(2)}) collective-permute-start(bf16[512,1024]{1,0:T(8,128)(2,1)} %fusion.16), channel_id=1, source_target_pairs={{0,1},{1,0},{2,3},{3,2},{4,5},{5,4},{6,7},{7,6},{8,9},{9,8},{10,11... | collective-permute-start | bytes 3145736 | tf_op jit(solution)/shard_map/ppermute | solution.py:230
  19.6 3.0 copy-start.12
  29.0 6.7 %copy-start.3 = (bf16[512,4096]{1,0:T(8,128)(2,1)S(1)}, bf16[512,4096]{1,0:T(8,128)(2,1)}, u32[]{:S(2)}) copy-start(bf16[512,4096]{1,0:T(8,128)(2,1)} %param.9) | copy-start | bytes 12582916
  29.0 6.7 %copy-start.5 = (bf16[512,1024]{1,0:T(8,128)(2,1)S(1)}, bf16[512,1024]{1,0:T(8,128)(2,1)}, u32[]{:S(2)}) copy-start(bf16[512,1024]{1,0:T(8,128)(2,1)} %param.10) | copy-start | bytes 3145732
  29.0 6.7 %copy-start.15 = (f32[1024]{0:T(1024)S(1)}, f32[1024]{0:T(1024)}, u32[]{:S(2)}) copy-start(f32[1024]{0:T(1024)} %param.12) | copy-start | bytes 12292
  32.3 26.9 %collective-permute-start.15 = (bf16[512,1024]{1,0:T(8,128)(2,1)S(1)}, bf16[512,1024]{1,0:T(8,128)(2,1)S(1)}, u32[]{:S(2)}, u32[]{:S(2)}) collective-permute-start(bf16[512,1024]{1,0:T(8,128)(2,1)S(1)} %add_convert_fusion), channel_id=1, source_target_pairs={{0,2},{1,3},{2,0},{3,1},{4,6},{5,7},{6,4},{7,5},{8,10},{9,11},{10,... | collective-permute-start | bytes 3145736 | tf_op jit(solution)/shard_map/ppermute | solution.py:232
  71.6 2.1 copy-start.2
  73.7 396.9 %all-to-all-start = ((bf16[32,528,128]{2,1,0:T(8,128)(2,1)}), bf16[32,528,128]{2,1,0:T(8,128)(2,1)}, u32[]{:S(2)}, u32[]{:S(2)}) async-start(bf16[32,528,128]{2,1,0:T(8,128)(2,1)} %copy-done.2), calls=%async_computation | async-start | bytes 8650752 | tf_op jit(solution)/shard_map/all_to_all | solution.py:264
  83.0 371.3 %all-reduce.4.cloned.1.call-start = ((), (), s32[]{:S(2)}) async-start(), calls=%async_computation.1 | async-start | bytes 270336
  86.0 67.9 %collective-permute-start.2 = (bf16[1024,512]{0,1:T(8,128)(2,1)}, bf16[1024,512]{0,1:T(8,128)(2,1)S(1)}, u32[]{:S(2)}, u32[]{:S(2)}) collective-permute-start(bf16[1024,512]{0,1:T(8,128)(2,1)} %convolution_convert_fusion.4), channel_id=1, source_target_pairs={{0,96},{4,100},{8,104},{12,108},{16,112},{20,116},{24,120},{28,124... | collective-permute-start | bytes 3145736 | tf_op jit(solution)/shard_map/ppermute | solution.py:174
  91.8 363.7 %collective-permute-start.1 = (bf16[1024,512]{0,1:T(8,128)(2,1)}, bf16[1024,512]{0,1:T(8,128)(2,1)S(1)}, u32[]{:S(2)}, u32[]{:S(2)}) collective-permute-start(bf16[1024,512]{0,1:T(8,128)(2,1)} %convolution_convert_fusion.5), channel_id=1, source_target_pairs={{0,32},{4,36},{8,40},{12,44},{16,48},{20,52},{24,56},{28,60},{32,6... | collective-permute-start | bytes 3145736 | tf_op jit(solution)/shard_map/ppermute | solution.py:174
  94.7 361.8 %collective-permute-start = (bf16[1024,512]{0,1:T(8,128)(2,1)}, bf16[1024,512]{0,1:T(8,128)(2,1)}, u32[]{:S(2)}, u32[]{:S(2)}) collective-permute-start(bf16[1024,512]{0,1:T(8,128)(2,1)} %convolution_convert_fusion.6), channel_id=1, source_target_pairs={{0,64},{4,68},{8,72},{12,76},{16,80},{20,84},{24,88},{28,92},{32,9... | collective-permute-start | bytes 3145736 | tf_op jit(solution)/shard_map/ppermute | solution.py:174
  102.1 364.1 %collective-permute-start.8 = (bf16[1024,512]{0,1:T(8,128)(2,1)}, bf16[1024,512]{0,1:T(8,128)(2,1)}, u32[]{:S(2)}, u32[]{:S(2)}) collective-permute-start(bf16[1024,512]{0,1:T(8,128)(2,1)} %convolution_convert_fusion), channel_id=1, source_target_pairs={{0,24},{4,28},{8,0},{12,4},{16,8},{20,12},{24,16},{28,20},{32,56},... | collective-permute-start | bytes 3145736 | tf_op jit(solution)/shard_map/ppermute | solution.py:175
  104.7 363.0 %collective-permute-start.7 = (bf16[1024,512]{0,1:T(8,128)(2,1)}, bf16[1024,512]{0,1:T(8,128)(2,1)}, u32[]{:S(2)}, u32[]{:S(2)}) collective-permute-start(bf16[1024,512]{0,1:T(8,128)(2,1)} %convolution_convert_fusion.1), channel_id=1, source_target_pairs={{0,8},{4,12},{8,16},{12,20},{16,24},{20,28},{24,0},{28,4},{32,40},... | collective-permute-start | bytes 3145736 | tf_op jit(solution)/shard_map/ppermute | solution.py:175
  107.1 49.3 %copy-start.16 = (u32[128]{0:T(128)S(1)}, u32[128]{0:T(128)}, u32[]{:S(2)}) copy-start(u32[128]{0:T(128)} %constant.191) | copy-start | bytes 1540
  153.9 313.8 %collective-permute-start.6 = (bf16[1024,512]{0,1:T(8,128)(2,1)}, bf16[1024,512]{0,1:T(8,128)(2,1)}, u32[]{:S(2)}, u32[]{:S(2)}) collective-permute-start(bf16[1024,512]{0,1:T(8,128)(2,1)} %convolution_convert_fusion.2), channel_id=1, source_target_pairs={{0,16},{4,20},{8,24},{12,28},{16,0},{20,4},{24,8},{28,12},{32,48},... | collective-permute-start | bytes 3145736 | tf_op jit(solution)/shard_map/ppermute | solution.py:175
  158.0 0.7 copy-start.6
  455.5 12.3 %copy-start.7 = (bf16[512,256]{1,0:T(8,128)(2,1)S(1)}, bf16[512,256]{1,0:T(8,128)(2,1)}, u32[]{:S(2)}) copy-start(bf16[512,256]{1,0:T(8,128)(2,1)} %get-tuple-element.26) | copy-start | bytes 786436
  455.5 12.3 %copy-start.8 = (bf16[512,256]{1,0:T(8,128)(2,1)S(1)}, bf16[512,256]{1,0:T(8,128)(2,1)}, u32[]{:S(2)}) copy-start(bf16[512,256]{1,0:T(8,128)(2,1)} %get-tuple-element.38) | copy-start | bytes 786436
  455.5 12.3 %copy-start.9 = (bf16[512,256]{1,0:T(8,128)(2,1)S(1)}, bf16[512,256]{1,0:T(8,128)(2,1)}, u32[]{:S(2)}) copy-start(bf16[512,256]{1,0:T(8,128)(2,1)} %get-tuple-element.39) | copy-start | bytes 786436
  455.5 12.3 %copy-start.10 = (bf16[512,256]{1,0:T(8,128)(2,1)S(1)}, bf16[512,256]{1,0:T(8,128)(2,1)}, u32[]{:S(2)}) copy-start(bf16[512,256]{1,0:T(8,128)(2,1)} %get-tuple-element.40) | copy-start | bytes 786436
  455.5 1.0 copy-start.14
  460.3 28.4 %collective-permute-start.5 = (bf16[256,512]{0,1:T(8,128)(2,1)}, bf16[256,512]{0,1:T(8,128)(2,1)}, u32[]{:S(2)}, u32[]{:S(2)}) collective-permute-start(bf16[256,512]{0,1:T(8,128)(2,1)} %get-tuple-element.48), channel_id=1, source_target_pairs={{0,24},{4,28},{8,0},{12,4},{16,8},{20,12},{24,16},{28,20},{32,56},... | collective-permute-start | bytes 786440 | tf_op jit(solution)/shard_map/ppermute | solution.py:182
  462.3 28.4 %collective-permute-start.4 = (bf16[256,512]{0,1:T(8,128)(2,1)}, bf16[256,512]{0,1:T(8,128)(2,1)}, u32[]{:S(2)}, u32[]{:S(2)}) collective-permute-start(bf16[256,512]{0,1:T(8,128)(2,1)} %get-tuple-element.49), channel_id=1, source_target_pairs={{0,8},{4,12},{8,16},{12,20},{16,24},{20,28},{24,0},{28,4},{32,40},... | collective-permute-start | bytes 786440 | tf_op jit(solution)/shard_map/ppermute | solution.py:182
  466.3 36.2 %collective-permute-start.3 = (bf16[256,512]{0,1:T(8,128)(2,1)}, bf16[256,512]{0,1:T(8,128)(2,1)}, u32[]{:S(2)}, u32[]{:S(2)}) collective-permute-start(bf16[256,512]{0,1:T(8,128)(2,1)} %get-tuple-element.47), channel_id=1, source_target_pairs={{0,16},{4,20},{8,24},{12,28},{16,0},{20,4},{24,8},{28,12},{32,48},... | collective-permute-start | bytes 786440 | tf_op jit(solution)/shard_map/ppermute | solution.py:182
  488.4 15.4 %collective-permute-start.16 = (bf16[1024,128]{1,0:T(8,128)(2,1)S(1)}, bf16[1024,128]{1,0:T(8,128)(2,1)S(1)}, u32[]{:S(2)}, u32[]{:S(2)}) collective-permute-start(bf16[1024,128]{1,0:T(8,128)(2,1)S(1)} %constant_dynamic-slice_fusion), channel_id=1, source_target_pairs={{0,1},{1,0},{2,3},{3,2},{4,5},{5,4},{6,7},{7,6},{8,9},{9,8},{10,11... | collective-permute-start | bytes 786440 | tf_op jit(solution)/shard_map/ppermute | solution.py:195
  488.6 18.4 %collective-permute-start.11 = (bf16[256,512]{0,1:T(8,128)(2,1)S(1)}, bf16[256,512]{0,1:T(8,128)(2,1)S(1)}, u32[]{:S(2)}, u32[]{:S(2)}) collective-permute-start(bf16[256,512]{0,1:T(8,128)(2,1)S(1)} %get-tuple-element.45), channel_id=1, source_target_pairs={{0,96},{4,100},{8,104},{12,108},{16,112},{20,116},{24,120},{28,124... | collective-permute-start | bytes 786440 | tf_op jit(solution)/shard_map/ppermute | solution.py:183
  488.7 19.0 %collective-permute-start.10 = (bf16[256,512]{0,1:T(8,128)(2,1)S(1)}, bf16[256,512]{0,1:T(8,128)(2,1)S(1)}, u32[]{:S(2)}, u32[]{:S(2)}) collective-permute-start(bf16[256,512]{0,1:T(8,128)(2,1)S(1)} %get-tuple-element.46), channel_id=1, source_target_pairs={{0,32},{4,36},{8,40},{12,44},{16,48},{20,52},{24,56},{28,60},{32,6... | collective-permute-start | bytes 786440 | tf_op jit(solution)/shard_map/ppermute | solution.py:183
  490.7 23.8 %collective-permute-start.9 = (bf16[256,512]{0,1:T(8,128)(2,1)S(1)}, bf16[256,512]{0,1:T(8,128)(2,1)S(1)}, u32[]{:S(2)}, u32[]{:S(2)}) collective-permute-start(bf16[256,512]{0,1:T(8,128)(2,1)S(1)} %get-tuple-element.44), channel_id=1, source_target_pairs={{0,64},{4,68},{8,72},{12,76},{16,80},{20,84},{24,88},{28,92},{32,9... | collective-permute-start | bytes 786440 | tf_op jit(solution)/shard_map/ppermute | solution.py:183
  503.9 11.0 %collective-permute-start.17 = (bf16[1024,128]{1,0:T(8,128)(2,1)S(1)}, bf16[1024,128]{1,0:T(8,128)(2,1)S(1)}, u32[]{:S(2)}, u32[]{:S(2)}) collective-permute-start(bf16[1024,128]{1,0:T(8,128)(2,1)S(1)} %add_convert_fusion.3), channel_id=1, source_target_pairs={{0,2},{1,3},{2,0},{3,1},{4,6},{5,7},{6,4},{7,5},{8,10},{9,11},{10,... | collective-permute-start | bytes 786440 | tf_op jit(solution)/shard_map/ppermute | solution.py:196
  514.7 7.7 %collective-permute-start.12 = (bf16[128,1024]{0,1:T(8,128)(2,1)S(1)}, bf16[128,1024]{0,1:T(8,128)(2,1)S(1)}, u32[]{:S(2)}, u32[]{:S(2)}) collective-permute-start(bf16[128,1024]{0,1:T(8,128)(2,1)S(1)} %fusion.71), channel_id=1, source_target_pairs={{0,4},{4,0},{8,12},{12,8},{16,20},{20,16},{24,28},{28,24},{32,36},... | collective-permute-start | bytes 786440 | tf_op jit(solution)/shard_map/ppermute | solution.py:187
  515.7 7.8 %collective-permute-start.18 = (f32[1024,128]{1,0:T(8,128)}, f32[1024,128]{1,0:T(8,128)S(1)}, u32[]{:S(2)}, u32[]{:S(2)}) collective-permute-start(f32[1024,128]{1,0:T(8,128)} %convert_add_fusion), channel_id=1, source_target_pairs={{0,1},{1,0},{2,3},{3,2},{4,5},{5,4},{6,7},{7,6},{8,9},{9,8},{10,11... | collective-permute-start | bytes 1572872 | tf_op jit(solution)/shard_map/ppermute | solution.py:197
  522.5 1.5 copy-start.13
  522.5 2.1 copy-start.4
  523.6 2.3 copy-start.1
Sparse Core Ops, SparseCore 0:
  158.8 295.3 all-reduce.3

commit v2 on v1

--- a/solution.py
+++ b/solution.py
@@ -11,8 +11,8 @@
 E = 128
 N_WIDE = 32
 CAP = 512
-ID_ROWS = 16
-BLOCK = CAP + ID_ROWS
+TAIL = 32
+BLOCK = CAP + TAIL
 N_ROWS = 2048
 HI = 4
 LO = N_ROWS // HI
@@ -44,10 +44,10 @@
     before = jnp.cumsum(block_total, axis=0) - block_total
     counted = (within + before[:, None, :]) * blocked.astype(F32)
     position = jnp.sum(counted, axis=2).reshape(entries).astype(jnp.int32)
-    return position, jnp.sum(block_total, axis=0)
-
-
-def scatter_kernel(slots_ref, base_ref, far_ref, ids_ref, out_ref, rows):
+    return position, jnp.sum(block_total, axis=0).astype(jnp.int32)
+
+
+def scatter_kernel(slots_ref, base_ref, far_ref, tail_ref, out_ref, rows):
     dump = N_WIDE * CAP
 
     def clear(i, _):
@@ -72,13 +72,13 @@
 
     def narrow_down(w, _):
         out_ref[w, :CAP, :] = rows[pl.ds(pl.multiple_of(w * CAP, CAP), CAP), :].astype(BF16)
-        out_ref[w, CAP:, :] = ids_ref[w]
+        out_ref[w, CAP:, :] = tail_ref[w]
         return 0
 
     lax.fori_loop(0, N_WIDE, narrow_down, 0)
 
 
-def scatter_entries(slots, base, far, ids):
+def scatter_entries(slots, base, far, tail):
     vmem = pl.BlockSpec(memory_space=pltpu.VMEM)
     return pl.pallas_call(
         scatter_kernel,
@@ -89,15 +89,16 @@
         compiler_params=pltpu.CompilerParams(vmem_limit_bytes=40 << 20),
         cost_estimate=pl.CostEstimate(flops=0, bytes_accessed=40 << 20, transcendentals=0),
         name="place_entries",
-    )(slots, base, far, ids)
-
-
-def sums_kernel(count_ref, recv_ref, out_ref, total):
+    )(slots, base, far, tail)
+
+
+def sums_kernel(count_ref, recv_ref, out_ref, bias_ref, total):
     total[...] = jnp.zeros_like(total)
+    bias_ref[...] = jnp.zeros_like(bias_ref)
     lane_rows = lax.broadcasted_iota(jnp.int32, (LO, E), 0)
 
     def add_half(w, half):
-        ids = recv_ref[w, CAP:, :].astype(F32)
+        ids = recv_ref[w, CAP : CAP + 16, :].astype(F32)
         row = (ids[0:4, :] * 64.0 + ids[4:8, :]).astype(jnp.int32) - 1
         hi = row // LO
         lo = row - hi * LO
@@ -121,6 +122,8 @@
 
     def source(w, _):
         count = count_ref[w]
+        sums = recv_ref[w, CAP:, :].astype(F32)
+        bias_ref[...] += sums[8:16, :] + sums[16:24, :]
         for half in range(2):
 
             @pl.when(count > half * 2 * E)
@@ -138,9 +141,9 @@
     vmem = pl.BlockSpec(memory_space=pltpu.VMEM)
     return pl.pallas_call(
         sums_kernel,
-        out_shape=jax.ShapeDtypeStruct((N_ROWS, E), BF16),
+        out_shape=(jax.ShapeDtypeStruct((N_ROWS, E), BF16), jax.ShapeDtypeStruct((8, E), F32)),
         in_specs=[pl.BlockSpec(memory_space=pltpu.SMEM), vmem],
-        out_specs=vmem,
+        out_specs=(vmem, vmem),
         scratch_shapes=[pltpu.VMEM((LO, HI * E), F32)],
         compiler_params=pltpu.CompilerParams(vmem_limit_bytes=40 << 20),
         cost_estimate=pl.CostEstimate(flops=8 << 30, bytes_accessed=5 << 20, transcendentals=0),
@@ -155,26 +158,61 @@
     return total
 
 
-def weight_grad_owned(embedded, scaled, z, y, x_lo):
+def terms_kernel(block_ref, embedded_ref, scaled_ref, *out_refs):
+    step = pl.program_id(0)
+    term = lax.dot_general(
+        embedded_ref[...], scaled_ref[...], (((0,), (0,)), ((), ())), preferred_element_type=F32
+    ).astype(BF16)
+    for q, out_ref in enumerate(out_refs):
+
+        @pl.when(step // 4 == q)
+        def _():
+            out_ref[...] = term
+
+
+def sent_terms(embedded, scaled, blocks):
+    samples, half = scaled.shape[0], scaled.shape[1] // 2
+
+    def out_map(q):
+        return lambda s, blocks: (jnp.clip(s - 4 * q, 0, 3), 0)
+
+    return pl.pallas_call(
+        terms_kernel,
+        out_shape=[jax.ShapeDtypeStruct((1024, half), BF16)] * 6,
+        grid_spec=pltpu.PrefetchScalarGridSpec(
+            num_scalar_prefetch=1,
+            grid=(24,),
+            in_specs=[
+                pl.BlockSpec((samples, 256), lambda s, blocks: (0, blocks[s])),
+                pl.BlockSpec((samples, half), lambda s, blocks: (0, s // 12)),
+            ],
+            out_specs=[pl.BlockSpec((256, half), out_map(q)) for q in range(6)],
+        ),
+        compiler_params=pltpu.CompilerParams(vmem_limit_bytes=32 << 20),
+        cost_estimate=pl.CostEstimate(flops=3 << 30, bytes_accessed=14 << 20, transcendentals=0),
+        name="sent_terms",
+    )(blocks, embedded, scaled)
+
+
+def weight_grad_owned(embedded, scaled, sent, z, y, x_lo):
     half = scaled.shape[1] // 2
     left, right = scaled[:, :half], scaled[:, half:]
     dims = (((0,), (0,)), ((), ()))
 
-    def term_z(d):
-        rows = lax.dynamic_slice_in_dim(embedded, ((z + d) % 4) * 1024, 1024, 1)
-        return lax.dot_general(rows, left, dims, preferred_element_type=F32).astype(BF16)
-
-    def term_y(d):
-        start = ((y + d) % 4) * 256
+    def term_z():
+        rows = lax.dynamic_slice_in_dim(embedded, z * 1024, 1024, 1)
+        return lax.dot_general(rows, left, dims, preferred_element_type=F32)
+
+    def term_y():
         rows = jnp.concatenate(
-            [lax.dynamic_slice_in_dim(embedded, k * 1024 + start, 256, 1) for k in range(4)], axis=1
+            [lax.dynamic_slice_in_dim(embedded, k * 1024 + y * 256, 256, 1) for k in range(4)], axis=1
         )
-        return lax.dot_general(rows, right, dims, preferred_element_type=F32).astype(BF16)
-
-    got_z = [lax.ppermute(term_z(d), "wide", z_perm(d)) for d in (2, 1, 3)]
-    got_y = [lax.ppermute(term_y(d), "wide", y_perm(d)) for d in (2, 1, 3)]
-    by_z = summed(term_z(0), got_z).astype(BF16)
-    by_y = summed(term_y(0), got_y).astype(BF16)
+        return lax.dot_general(rows, right, dims, preferred_element_type=F32)
+
+    got_z = [lax.ppermute(sent[q], "wide", z_perm(d)) for q, d in enumerate((2, 1, 3))]
+    got_y = [lax.ppermute(sent[3 + q], "wide", y_perm(d)) for q, d in enumerate((2, 1, 3))]
+    by_z = summed(term_z(), got_z).astype(BF16)
+    by_y = summed(term_y(), got_y).astype(BF16)
 
     def piece(array, at):
         return lax.dynamic_slice_in_dim(array, (at % 4) * 256, 256, 0)
@@ -229,7 +267,14 @@
 
     from_mate_far = lax.ppermute(backward_part(3).astype(BF16), "narrow", CORE)
     chip_far = (backward_part(2) + from_mate_far.astype(F32)).astype(BF16)
+    chip_far, scaled, embedded = lax.optimization_barrier((chip_far, scaled, embedded))
     far = lax.ppermute(chip_far, "narrow", X_HI)
+    column_blocks = jnp.stack(
+        [((z + d) % 4) * 4 + k for d in (2, 1, 3) for k in range(4)]
+        + [k * 4 + (y + d) % 4 for d in (2, 1, 3) for k in range(4)]
+    )
+    sent = sent_terms(embedded, scaled, column_blocks)
+    embedded, *sent = lax.optimization_barrier((embedded, *sent))
     from_mate = lax.ppermute(backward_part(1).astype(BF16), "narrow", CORE)
     cross_out = jnp.dot(embedded, cross_weight, preferred_element_type=F32) + cross_bias
     base = grad_out + grad_out * cross_out + backward_part(0) + from_mate.astype(F32)
@@ -253,20 +298,30 @@
     at_position = (position[:, None] == jnp.arange(CAP, dtype=jnp.int32)[None, :]).astype(BF16)
     ids = lax.dot_general(halves, at_position, (((0,), (0,)), ((), ())), preferred_element_type=F32)
     ids = ids.astype(BF16).reshape(2, N_WIDE, CAP // E, E).transpose(1, 0, 2, 3)
-    ids = jnp.pad(ids.reshape(N_WIDE, 2 * CAP // E, E), ((0, 0), (0, ID_ROWS - 2 * CAP // E), (0, 0)))
 
     bias_part = jnp.sum(scaled, axis=0, dtype=F32)
-    shared = lax.all_gather(jnp.concatenate([bias_part, counts]), "wide")
-    bias_grad = jnp.sum(shared[:, :width], axis=0) * norm_factor
-    recv_counts = lax.dynamic_slice_in_dim(shared, width + wide, 1, 1).reshape(-1).astype(jnp.int32)
-
-    payload = scatter_entries(slots, base, far, ids)
+    bias_top = lax.reduce_precision(bias_part, 8, 7)
+    bias_parts = jnp.stack([bias_top, bias_part - bias_top]).astype(BF16).reshape(1, 16, E)
+    count_parts = jnp.stack([counts // 64, counts % 64], axis=1).astype(BF16)
+    tail = jnp.concatenate(
+        [
+            ids.reshape(N_WIDE, 8, E),
+            jnp.broadcast_to(bias_parts, (N_WIDE, 16, E)),
+            jnp.broadcast_to(jnp.repeat(count_parts, 4, axis=1)[:, :, None], (N_WIDE, 8, E)),
+        ],
+        axis=1,
+    )
+
+    payload = scatter_entries(slots, base, far, tail)
     recv = lax.all_to_all(payload, "wide", split_axis=0, concat_axis=0, tiled=True)
-    row_grad = over_narrow(owned_sums(recv_counts, recv), core)
+    recv_counts = (recv[:, CAP + 24, 0].astype(F32) * 64.0 + recv[:, CAP + 28, 0].astype(F32)).astype(jnp.int32)
+    sums, bias_sums = owned_sums(recv_counts, recv)
+    bias_grad = bias_sums.reshape(-1) * norm_factor
+    row_grad = over_narrow(sums, core)
     new_state = adagrad_state + jnp.mean(row_grad * row_grad, axis=1)
     new_table = emb_table - LEARN_RATE * row_grad / jnp.sqrt(new_state)[:, None]
 
-    weight_grad = weight_grad_owned(embedded, scaled, z, y, x_lo) * norm_factor
+    weight_grad = weight_grad_owned(embedded, scaled, sent, z, y, x_lo) * norm_factor
     return (weight_grad, bias_grad, new_table, new_state)
 
 

time: 538 us -> 262 us (0.49)
  waiting for transfers between devices: 369 us -> 117 us
  matrix products: 44.5 us -> 30.3 us
  between operations: 15.4 us -> 1.39 us
  Pallas kernels: 30.1 us -> 40.9 us
  local copies, waits for them, and re-layouts: 14.8 us -> 8.82 us
    unnamed x2 -> x0, waiting for transfers between devices: 295 us -> none
    ppermute x6, waiting for transfers between devices: 45.1 us -> 83.4 us  [the longest x3 83.4 us: weight_grad_owned(): lax.ppermute(sent[q], 'wide', z_perm(d))]
    ppermute x1, starting transfers between devices: 0.09 us -> 16.7 us  [weight_grad_owned(): lax.ppermute(lax.dynamic_slice_in_dim(pair, (1 - x_lo) * E, E, 0), 'wide'...]
    dot_general x8 -> x2, matrix products: 19.7 us -> 5.89 us  [the longest x1 3.1 us: term_z(): return lax.dot_general(rows, left, dims, preferred_element_type=F32)]
    pallas_call x1 -> x2, Pallas kernels: 17.7 us -> 28.5 us  [the longest x1 17.7 us: owned_sums(): pl.pallas_call(sums_kernel, out_shape=(jax.ShapeDtypeStruct((N_ROWS, E),...]
    ppermute x3, starting transfers between devices: 13.9 us -> 3.31 us  [weight_grad_owned(): lax.ppermute(piece(by_y, z + d), 'wide', z_perm(d))]
  transfers between devices with their start and end apart: 21 -> 20, of which waited for: 6 -> 6; matrix products, arithmetic and copies ran while one was open for 11% -> 13% of each run, Pallas kernels for 3% -> 7%
where the time goes in v2:
time: 262 us; the launch traced here: 260 us
  waiting for transfers between devices  117 us (45%)
  starting transfers between devices  50.2 us (19%)
  Pallas kernels  40.9 us (16%)
  matrix products  30.3 us (12%)
  other arithmetic  11.2 us (4%)
  local copies, waits for them, and re-layouts  8.82 us (3%)
    ppermute x3, waiting for transfers between devices, weight_grad_owned(): lax.ppermute(sent[q], 'wide', z_perm(d))  83.4 us
    ppermute x1, waiting for transfers between devices, body(): far = lax.ppermute(chip_far, 'narrow', X_HI)  19 us
    pallas_call x1, Pallas kernels, owned_sums(): pl.pallas_call(sums_kernel, out_shape=(jax.ShapeDtypeStruct((N_ROWS, E),...  17.7 us
    ppermute x1, starting transfers between devices, weight_grad_owned(): lax.ppermute(lax.dynamic_slice_in_dim(pair, (1 - x_lo) * E, E, 0), 'wide'...  16.7 us
    dot_general x4, matrix products, backward_part(): lax.dot_general(scaled, rows, (((1,), (1,)), ((), ())), preferred_element...  15.1 us
    pallas_call x1, Pallas kernels, scatter_entries(): pl.pallas_call(scatter_kernel, out_shape=jax.ShapeDtypeStruct((N_WIDE, BL...  12.4 us
    pallas_call x1, Pallas kernels, sent_terms(): pl.pallas_call(terms_kernel, out_shape=[jax.ShapeDtypeStruct((1024, half)...  10.8 us
    all_to_all x1, starting transfers between devices, body(): lax.all_to_all(payload, 'wide', split_axis=0, concat_axis=0, tiled=True)  9.43 us
  transfers between devices with their start and end apart: 20, of which 6 were waited for; matrix products, arithmetic and copies ran while one was open for 13% of the time, Pallas kernels for 7%

profile of v2, /device:TPU:24, one launch (start us, length us, event | category | flops | bytes accessed | tf_op | source)
XLA Modules:
  0.0 260.2 jit_solution(15913627719565327507)
XLA Ops:
  0.7 2.0 fusion.2.scaled_ref
  2.6 3.9 %fusion.13 = bf16[512,1024]{1,0:T(8,128)(2,1)} fusion(bf16[512,1024]{1,0:T(8,128)(2,1)S(1)} %fusion.2.scaled_ref, bf16[4096,1024]{1,0:T(8,128)(2,1)} %param.11, s32[]{:T(128)S(6)} %select_n.248), kind=kOutput, calls=%fused_computation.24 | convolution fusion | flops 1074266112 | bytes 4194308 | tf_op jit(solution)/shard_map/dot_general | solution.py:266
  6.7 1.3 iota_compare_fusion.2
  8.0 1.6 lt.230
  9.6 1.6 lt.231
  11.6 0.3 convert_reduce_fusion.1
  11.9 0.6 fusion.24
  13.4 2.9 %fusion.25 = bf16[64,512]{1,0:T(8,128)(2,1)S(1)} fusion(s32[8192]{0:T(1024)S(1)} %bitcast.76, bf16[8192,32]{0,1:T(8,128)(2,1)S(1)} %get-tuple-element.59, bf16[8192,32]{0,1:T(8,128)(2,1)S(1)} %get-tuple-element.58), kind=kOutput, calls=%fused_computation.29 | convolution fusion | flops 543195136 | bytes 1146880 | tf_op jit(solution)/shard_map/dot_general | solution.py:299
  16.5 4.3 %add_convert_fusion.2 = bf16[512,1024]{1,0:T(8,128)(2,1)} fusion(bf16[512,1024]{1,0:T(8,128)(2,1)} %collective-permute-done, bf16[512,1024]{1,0:T(8,128)(2,1)S(1)} %fusion.2.scaled_ref, bf16[4096,1024]{1,0:T(8,128)(2,1)} %param.11, s32[]{:T(128)S(6)} %select_n.247), kind=kOutput, calls=%fused_computation.16 | convolution fusion | flops 1075314688 | bytes 5242884 | tf_op jit(solution)/shard_map/dot_general | solution.py:266
  20.8 10.8 %sent_terms.1 = (bf16[1024,512]{1,0:T(8,128)(2,1)S(1)}, bf16[1024,512]{1,0:T(8,128)(2,1)S(1)}, bf16[1024,512]{1,0:T(8,128)(2,1)S(1)}, bf16[1024,512]{1,0:T(8,128...) custom-call(s32[24]{0:T(128)S(1)} %stack.111.block_ref, bf16[512,4096]{1,0:T(8,128)(2,1)S(1)} %copy-done.2, ...), custom_call_target="tpu_custom_call" | custom-call | flops 3221225472 | bytes 14680064 | tf_op jit(solution)/shard_map/sent_terms/pallas_call | solution.py:179
  31.7 2.6 %fusion.16 = bf16[512,1024]{1,0:T(8,128)(2,1)} fusion(bf16[512,1024]{1,0:T(8,128)(2,1)S(1)} %fusion.2.scaled_ref, bf16[4096,1024]{1,0:T(8,128)(2,1)S(1)} %bitcast.80, s32[]{:T(128)S(6)} %select_n.280), kind=kOutput, calls=%fused_computation.25 | convolution fusion | flops 1074266112 | bytes 4194308 | tf_op jit(solution)/shard_map/dot_general | solution.py:266
  34.4 0.8 collective-permute-start.14
  35.1 5.8 %fusion.68 = f32[512,1024]{1,0:T(8,128)} fusion(bf16[512,4096]{1,0:T(8,128)(2,1)S(1)} %copy-done.2, bf16[4096,1024]{1,0:T(8,128)(2,1)S(1)} %bitcast.80), kind=kOutput, calls=%fused_computation.124 | convolution fusion | flops 4294967296 | bytes 14680064 | tf_op jit(solution)/shard_map/dot_general | solution.py:279
  41.0 3.0 %collective-permute-start.15 = (bf16[512,1024]{1,0:T(8,128)(2,1)}, bf16[512,1024]{1,0:T(8,128)(2,1)S(1)}, u32[]{:S(2)}, u32[]{:S(2)}) collective-permute-start(bf16[512,1024]{1,0:T(8,128)(2,1)} %add_convert_fusion.2), channel_id=1, source_target_pairs={{0,2},{1,3},{2,0},{3,1},{4,6},{5,7},{6,4},{7,5},{8,10},{9,11},{10,... | collective-permute-start | bytes 3145736 | tf_op jit(solution)/shard_map/ppermute | solution.py:271
  44.4 4.3 %fusion.4.base_ref = f32[512,1024]{1,0:T(8,128)S(1)} fusion(bf16[512,1024]{1,0:T(8,128)(2,1)} %param.10, bf16[512,1024]{1,0:T(8,128)(2,1)} %collective-permute-done.14, f32[512,1024]{1,0:T(8,128)} %fusion.68, bf16[512,1024]{1,0:T(8,128)(2,1)S(1)} %fusion.2.scaled_ref, bf16[4096,1024]{1,0:T(8,128)(2,1)} %param.11, s32[]{:T(128)S(6)} %select_n.246, ...), kind=kOutput, calls=%fused_computation.7 | convolution fusion | flops 1077411840 | bytes 9441284 | tf_op jit(solution)/shard_map/dot_general | solution.py:266
  48.7 19.0 %collective-permute-done.15.far_ref = bf16[512,1024]{1,0:T(8,128)(2,1)S(1)} collective-permute-done((bf16[512,1024]{1,0:T(8,128)(2,1)}, bf16[512,1024]{1,0:T(8,128)(2,1)S(1)}, u32[]{:S(2)}, u32[]{:S(2)}) %collective-permute-start.15) | collective-permute-done | bytes 1048608 | tf_op jit(solution)/shard_map/ppermute | solution.py:271
  67.8 12.4 %place_entries.1 = bf16[32,544,128]{2,1,0:T(8,128)(2,1)S(1)} custom-call(s32[8192]{0:T(1024)S(1)} %get-tuple-element.57.slots_ref, f32[512,1024]{1,0:T(8,128)S(1)} %fusion.4.base_ref, bf16[512,1024]{1,0:T(8,128)(2,1)S(1)} %collective-permute-done.15.far_ref, bf16[32,32,128]{2,1,0:T(8,128)(2,1)S(1)} %pad_maximum_fusion.1.tail_ref), custom_call_target="tpu_custom_call" | custom-call | bytes 41943040 | tf_op jit(solution)/shard_map/place_entries/pallas_call | solution.py:83
  80.2 2.1 copy-done.1
  82.3 9.4 %all-to-all-start = ((bf16[32,544,128]{2,1,0:T(8,128)(2,1)}), bf16[32,544,128]{2,1,0:T(8,128)(2,1)}, u32[]{:S(2)}, u32[]{:S(2)}) async-start(bf16[32,544,128]{2,1,0:T(8,128)(2,1)} %copy-done.1), calls=%async_computation | async-start | bytes 8912896 | tf_op jit(solution)/shard_map/all_to_all | solution.py:316
  91.7 2.8 %collective-permute-start.3 = (bf16[1024,512]{1,0:T(8,128)(2,1)}, bf16[1024,512]{1,0:T(8,128)(2,1)}, u32[]{:S(2)}, u32[]{:S(2)}) collective-permute-start(bf16[1024,512]{1,0:T(8,128)(2,1)} %copy-done.8), channel_id=1, source_target_pairs={{0,96},{4,100},{8,104},{12,108},{16,112},{20,116},{24,120},{28,124... | collective-permute-start | bytes 3145736 | tf_op jit(solution)/shard_map/ppermute | solution.py:212
  94.5 2.3 collective-permute-start.1
  96.8 0.8 collective-permute-start.9
  97.6 2.4 collective-permute-start.8
  100.0 64.1 %collective-permute-done.3 = bf16[1024,512]{1,0:T(8,128)(2,1)} collective-permute-done((bf16[1024,512]{1,0:T(8,128)(2,1)}, bf16[1024,512]{1,0:T(8,128)(2,1)}, u32[]{:S(2)}, u32[]{:S(2)}) %collective-permute-start.3) | collective-permute-done | bytes 1048608 | tf_op jit(solution)/shard_map/ppermute | solution.py:212
  164.1 2.5 collective-permute-start.7
  166.6 1.3 constant_dynamic-slice_fusion.8
  167.9 19.3 %collective-permute-done.1 = bf16[1024,512]{1,0:T(8,128)(2,1)} collective-permute-done((bf16[1024,512]{1,0:T(8,128)(2,1)}, bf16[1024,512]{1,0:T(8,128)(2,1)}, u32[]{:S(2)}, u32[]{:S(2)}) %collective-permute-start.1) | collective-permute-done | bytes 1048608 | tf_op jit(solution)/shard_map/ppermute | solution.py:212
  187.2 3.1 %add_convert_fusion.1 = bf16[1024,512]{1,0:T(8,128)(2,1)S(1)} fusion(bf16[1024,512]{1,0:T(8,128)(2,1)} %collective-permute-done.3, bf16[1024,512]{1,0:T(8,128)(2,1)} %collective-permute-done.2, bf16[1024,512]{1,0:T(8,128)(2,1)} %collective-permute-done.1, bf16[512,4096]{1,0:T(8,128)(2,1)} %embedded_ref, s32[]{:T(128)S(6)} %select_n.258, ...), kind=kOutput, calls=%fused_computation.15 | convolution fusion | flops 540540928 | bytes 5767172 | tf_op jit(solution)/shard_map/dot_general | solution.py:204
  190.3 1.0 constant_dynamic-slice_fusion.11
  191.3 1.2 collective-permute-start.6
  192.5 2.0 collective-permute-start.5
  194.7 2.8 %add_convert_fusion = bf16[1024,512]{1,0:T(8,128)(2,1)S(1)} fusion(bf16[1024,512]{1,0:T(8,128)(2,1)} %collective-permute-done.9, bf16[1024,512]{1,0:T(8,128)(2,1)} %collective-permute-done.8, bf16[1024,512]{1,0:T(8,128)(2,1)} %collective-permute-done.7, bf16[512,256]{1,0:T(8,128)(2,1)S(1)} %get-tuple-element.45, ...), kind=kOutput, calls=%fused_computation.14 | convolution fusion | flops 544735232 | bytes 5767168 | tf_op jit(solution)/shard_map/dot_general | solution.py:210
  197.5 1.6 fusion.56.count_ref
  199.1 17.7 %owned_sums.1 = (bf16[2048,128]{1,0:T(8,128)(2,1)S(1)}, f32[8,128]{1,0:T(8,128)S(1)}) custom-call(s32[32]{0:T(128)S(1)} %fusion.56.count_ref, bf16[32,544,128]{2,1,0:T(8,128)(2,1)} %all-to-all-done.recv_ref), custom_call_target="tpu_custom_call" | custom-call | flops 8589934592 | bytes 5242880 | tf_op jit(solution)/shard_map/owned_sums/pallas_call | solution.py:142
  216.9 1.1 collective-permute-start.12
  218.1 1.0 collective-permute-start.11
  219.0 1.2 collective-permute-start.10
  220.3 1.3 add_convert_fusion.5
  221.7 2.6 %collective-permute-start.17 = (bf16[1024,128]{1,0:T(8,128)(2,1)S(1)}, bf16[1024,128]{1,0:T(8,128)(2,1)S(1)}, u32[]{:S(2)}, u32[]{:S(2)}) collective-permute-start(bf16[1024,128]{1,0:T(8,128)(2,1)S(1)} %add_convert_fusion.3), channel_id=1, source_target_pairs={{0,2},{1,3},{2,0},{3,1},{4,6},{5,7},{6,4},{7,5},{8,10},{9,11},{10,... | collective-permute-start | bytes 786440 | tf_op jit(solution)/shard_map/ppermute | solution.py:234
  224.3 1.8 collective-permute-done.12
  226.1 7.2 %collective-permute-done.11 = bf16[256,512]{1,0:T(8,128)(2,1)S(1)} collective-permute-done((bf16[256,512]{1,0:T(8,128)(2,1)S(1)}, bf16[256,512]{1,0:T(8,128)(2,1)S(1)}, u32[]{:S(2)}, u32[]{:S(2)}) %collective-permute-start.11) | collective-permute-done | bytes 262176 | tf_op jit(solution)/shard_map/ppermute | solution.py:221
  233.5 16.7 %collective-permute-start.13 = (bf16[128,1024]{1,0:T(8,128)(2,1)S(1)}, bf16[128,1024]{1,0:T(8,128)(2,1)S(1)}, u32[]{:S(2)}, u32[]{:S(2)}) collective-permute-start(bf16[128,1024]{1,0:T(8,128)(2,1)S(1)} %fusion.49), channel_id=1, source_target_pairs={{0,4},{4,0},{8,12},{12,8},{16,20},{20,16},{24,28},{28,24},{32,36},... | collective-permute-start | bytes 786440 | tf_op jit(solution)/shard_map/ppermute | solution.py:225
  250.4 6.0 %collective-permute-done.13 = bf16[128,1024]{1,0:T(8,128)(2,1)S(1)} collective-permute-done((bf16[128,1024]{1,0:T(8,128)(2,1)S(1)}, bf16[128,1024]{1,0:T(8,128)(2,1)S(1)}, u32[]{:S(2)}, u32[]{:S(2)}) %collective-permute-start.13) | collective-permute-done | bytes 262176 | tf_op jit(solution)/shard_map/ppermute | solution.py:225
  256.3 0.9 add_multiply_fusion
  257.2 0.6 multiply_bitcast_fusion
  257.9 0.3 multiply_reduce_fusion
  258.3 0.6 fusion.67
  258.9 1.3 divide_subtract_fusion
  (90 shorter events, 2.6 us)
Async XLA Ops:
  0.6 5.9 %copy-start = (s32[512,32]{0,1:T(8,128)S(1)}, s32[512,32]{0,1:T(8,128)}, u32[]{:S(2)}) copy-start(s32[512,32]{0,1:T(8,128)} %param.13) | copy-start | bytes 196612
  6.5 4.7 %copy-start.11 = (s32[1,512,16,1]{1,3,2,0:T(1,128)S(1)}, s32[1,512,16,1]{1,3,2,0:T(1,128)}, u32[]{:S(2)}) copy-start(s32[1,512,16,1]{1,3,2,0:T(1,128)} %param.14) | copy-start | bytes 98308
  6.5 10.0 %collective-permute-start = (bf16[512,1024]{1,0:T(8,128)(2,1)}, bf16[512,1024]{1,0:T(8,128)(2,1)}, u32[]{:S(2)}, u32[]{:S(2)}) collective-permute-start(bf16[512,1024]{1,0:T(8,128)(2,1)} %fusion.13), channel_id=1, source_target_pairs={{0,1},{1,0},{2,3},{3,2},{4,5},{5,4},{6,7},{7,6},{8,9},{9,8},{10,11... | collective-permute-start | bytes 3145736 | tf_op jit(solution)/shard_map/ppermute | solution.py:268
  9.6 3.0 %copy-start.12 = (s32[1,512,16]{1,2,0:T(8,128)S(1)}, s32[1,512,16]{1,2,0:T(8,128)}, u32[]{:S(2)}) copy-start(s32[1,512,16]{1,2,0:T(8,128)} %param.15) | copy-start | bytes 98308
  16.4 4.4 %copy-start.2 = (bf16[512,4096]{1,0:T(8,128)(2,1)S(1)}, bf16[512,4096]{1,0:T(8,128)(2,1)}, u32[]{:S(2)}) copy-start(bf16[512,4096]{1,0:T(8,128)(2,1)} %embedded_ref) | copy-start | bytes 12582916
  16.5 15.3 %slice-start = ((s8[8388608]{0:T(1024)(128)(4,1)}), s8[4194304]{0:T(1024)(128)(4,1)S(1)}, s32[]{:S(2)}) async-start(s8[8388608]{0:T(1024)(128)(4,1)} %bitcast.79), calls=%async_computation.1 | async-start | bytes 8388608
  20.8 10.9 %slice-start.1 = ((s8[8388608]{0:T(1024)(128)(4,1)}), s8[4194304]{0:T(1024)(128)(4,1)S(1)}, s32[]{:S(2)}) async-start(s8[8388608]{0:T(1024)(128)(4,1)} %bitcast.79), calls=%async_computation.2 | async-start | bytes 8388608
  31.7 2.7 %copy-start.3 = (bf16[1024,512]{1,0:T(8,128)(2,1)}, bf16[1024,512]{1,0:T(8,128)(2,1)S(1)}, u32[]{:S(2)}) copy-start(bf16[1024,512]{1,0:T(8,128)(2,1)S(1)} %get-tuple-element.35) | copy-start | bytes 3145732
  31.7 2.7 %copy-start.5 = (bf16[1024,512]{1,0:T(8,128)(2,1)}, bf16[1024,512]{1,0:T(8,128)(2,1)S(1)}, u32[]{:S(2)}) copy-start(bf16[1024,512]{1,0:T(8,128)(2,1)S(1)} %get-tuple-element.36) | copy-start | bytes 3145732
  31.7 2.7 %copy-start.6 = (bf16[1024,512]{1,0:T(8,128)(2,1)}, bf16[1024,512]{1,0:T(8,128)(2,1)S(1)}, u32[]{:S(2)}) copy-start(bf16[1024,512]{1,0:T(8,128)(2,1)S(1)} %get-tuple-element.31) | copy-start | bytes 3145732
  31.7 2.7 %copy-start.7 = (bf16[1024,512]{1,0:T(8,128)(2,1)}, bf16[1024,512]{1,0:T(8,128)(2,1)S(1)}, u32[]{:S(2)}) copy-start(bf16[1024,512]{1,0:T(8,128)(2,1)S(1)} %get-tuple-element.32) | copy-start | bytes 3145732
  31.7 2.7 %copy-start.8 = (bf16[1024,512]{1,0:T(8,128)(2,1)}, bf16[1024,512]{1,0:T(8,128)(2,1)S(1)}, u32[]{:S(2)}) copy-start(bf16[1024,512]{1,0:T(8,128)(2,1)S(1)} %get-tuple-element.33) | copy-start | bytes 3145732
  34.4 10.0 %copy-start.14 = (f32[1024]{0:T(1024)S(1)}, f32[1024]{0:T(1024)}, u32[]{:S(2)}) copy-start(f32[1024]{0:T(1024)} %param.12) | copy-start | bytes 12292
  34.4 10.0 %collective-permute-start.14 = (bf16[512,1024]{1,0:T(8,128)(2,1)}, bf16[512,1024]{1,0:T(8,128)(2,1)}, u32[]{:S(2)}, u32[]{:S(2)}) collective-permute-start(bf16[512,1024]{1,0:T(8,128)(2,1)} %fusion.16), channel_id=1, source_target_pairs={{0,1},{1,0},{2,3},{3,2},{4,5},{5,4},{6,7},{7,6},{8,9},{9,8},{10,11... | collective-permute-start | bytes 3145736 | tf_op jit(solution)/shard_map/ppermute | solution.py:278
  41.0 26.8 %collective-permute-start.15 = (bf16[512,1024]{1,0:T(8,128)(2,1)}, bf16[512,1024]{1,0:T(8,128)(2,1)S(1)}, u32[]{:S(2)}, u32[]{:S(2)}) collective-permute-start(bf16[512,1024]{1,0:T(8,128)(2,1)} %add_convert_fusion.2), channel_id=1, source_target_pairs={{0,2},{1,3},{2,0},{3,1},{4,6},{5,7},{6,4},{7,5},{8,10},{9,11},{10,... | collective-permute-start | bytes 3145736 | tf_op jit(solution)/shard_map/ppermute | solution.py:271
  80.2 2.1 copy-start.1
  82.3 15.4 %copy-start.4 = (bf16[1024,512]{1,0:T(8,128)(2,1)S(1)}, bf16[1024,512]{1,0:T(8,128)(2,1)}, u32[]{:S(2)}) copy-start(bf16[1024,512]{1,0:T(8,128)(2,1)} %copy-done.3) | copy-start | bytes 3145732
  82.3 115.2 %all-to-all-start = ((bf16[32,544,128]{2,1,0:T(8,128)(2,1)}), bf16[32,544,128]{2,1,0:T(8,128)(2,1)}, u32[]{:S(2)}, u32[]{:S(2)}) async-start(bf16[32,544,128]{2,1,0:T(8,128)(2,1)} %copy-done.1), calls=%async_computation | async-start | bytes 8912896 | tf_op jit(solution)/shard_map/all_to_all | solution.py:316
  91.7 72.4 %collective-permute-start.3 = (bf16[1024,512]{1,0:T(8,128)(2,1)}, bf16[1024,512]{1,0:T(8,128)(2,1)}, u32[]{:S(2)}, u32[]{:S(2)}) collective-permute-start(bf16[1024,512]{1,0:T(8,128)(2,1)} %copy-done.8), channel_id=1, source_target_pairs={{0,96},{4,100},{8,104},{12,108},{16,112},{20,116},{24,120},{28,124... | collective-permute-start | bytes 3145736 | tf_op jit(solution)/shard_map/ppermute | solution.py:212
  94.5 73.3 %collective-permute-start.2 = (bf16[1024,512]{1,0:T(8,128)(2,1)}, bf16[1024,512]{1,0:T(8,128)(2,1)}, u32[]{:S(2)}, u32[]{:S(2)}) collective-permute-start(bf16[1024,512]{1,0:T(8,128)(2,1)} %copy-done.7), channel_id=1, source_target_pairs={{0,32},{4,36},{8,40},{12,44},{16,48},{20,52},{24,56},{28,60},{32,6... | collective-permute-start | bytes 3145736 | tf_op jit(solution)/shard_map/ppermute | solution.py:212
  94.5 92.7 %collective-permute-start.1 = (bf16[1024,512]{1,0:T(8,128)(2,1)}, bf16[1024,512]{1,0:T(8,128)(2,1)}, u32[]{:S(2)}, u32[]{:S(2)}) collective-permute-start(bf16[1024,512]{1,0:T(8,128)(2,1)} %copy-done.6), channel_id=1, source_target_pairs={{0,64},{4,68},{8,72},{12,76},{16,80},{20,84},{24,88},{28,92},{32,9... | collective-permute-start | bytes 3145736 | tf_op jit(solution)/shard_map/ppermute | solution.py:212
  96.8 97.8 %collective-permute-start.9 = (bf16[1024,512]{1,0:T(8,128)(2,1)}, bf16[1024,512]{1,0:T(8,128)(2,1)}, u32[]{:S(2)}, u32[]{:S(2)}) collective-permute-start(bf16[1024,512]{1,0:T(8,128)(2,1)} %copy-done.5), channel_id=1, source_target_pairs={{0,24},{4,28},{8,0},{12,4},{16,8},{20,12},{24,16},{28,20},{32,56},... | collective-permute-start | bytes 3145736 | tf_op jit(solution)/shard_map/ppermute | solution.py:213
  97.6 97.0 %collective-permute-start.8 = (bf16[1024,512]{1,0:T(8,128)(2,1)S(1)}, bf16[1024,512]{1,0:T(8,128)(2,1)}, u32[]{:S(2)}, u32[]{:S(2)}) collective-permute-start(bf16[1024,512]{1,0:T(8,128)(2,1)S(1)} %copy-done.4), channel_id=1, source_target_pairs={{0,8},{4,12},{8,16},{12,20},{16,24},{20,28},{24,0},{28,4},{32,40},... | collective-permute-start | bytes 3145736 | tf_op jit(solution)/shard_map/ppermute | solution.py:213
  164.1 30.6 %collective-permute-start.7 = (bf16[1024,512]{1,0:T(8,128)(2,1)S(1)}, bf16[1024,512]{1,0:T(8,128)(2,1)}, u32[]{:S(2)}, u32[]{:S(2)}) collective-permute-start(bf16[1024,512]{1,0:T(8,128)(2,1)S(1)} %get-tuple-element.34), channel_id=1, source_target_pairs={{0,16},{4,20},{8,24},{12,28},{16,0},{20,4},{24,8},{28,12},{32,48},... | collective-permute-start | bytes 3145736 | tf_op jit(solution)/shard_map/ppermute | solution.py:213
  190.3 4.4 %copy-start.10 = (bf16[1024,512]{1,0:T(8,128)(2,1)}, bf16[1024,512]{1,0:T(8,128)(2,1)S(1)}, u32[]{:S(2)}) copy-start(bf16[1024,512]{1,0:T(8,128)(2,1)S(1)} %add_convert_fusion.1) | copy-start | bytes 3145732
  191.3 26.7 %collective-permute-start.6 = (bf16[256,512]{1,0:T(8,128)(2,1)}, bf16[256,512]{1,0:T(8,128)(2,1)}, u32[]{:S(2)}, u32[]{:S(2)}) collective-permute-start(bf16[256,512]{1,0:T(8,128)(2,1)} %get-tuple-element.54), channel_id=1, source_target_pairs={{0,24},{4,28},{8,0},{12,4},{16,8},{20,12},{24,16},{28,20},{32,56},... | collective-permute-start | bytes 786440 | tf_op jit(solution)/shard_map/ppermute | solution.py:220
  192.5 26.5 %collective-permute-start.5 = (bf16[256,512]{1,0:T(8,128)(2,1)}, bf16[256,512]{1,0:T(8,128)(2,1)}, u32[]{:S(2)}, u32[]{:S(2)}) collective-permute-start(bf16[256,512]{1,0:T(8,128)(2,1)} %get-tuple-element.55), channel_id=1, source_target_pairs={{0,8},{4,12},{8,16},{12,20},{16,24},{20,28},{24,0},{28,4},{32,40},... | collective-permute-start | bytes 786440 | tf_op jit(solution)/shard_map/ppermute | solution.py:220
  194.5 25.7 %collective-permute-start.4 = (bf16[256,512]{1,0:T(8,128)(2,1)S(1)}, bf16[256,512]{1,0:T(8,128)(2,1)}, u32[]{:S(2)}, u32[]{:S(2)}) collective-permute-start(bf16[256,512]{1,0:T(8,128)(2,1)S(1)} %get-tuple-element.53), channel_id=1, source_target_pairs={{0,16},{4,20},{8,24},{12,28},{16,0},{20,4},{24,8},{28,12},{32,48},... | collective-permute-start | bytes 786440 | tf_op jit(solution)/shard_map/ppermute | solution.py:220
  216.8 4.8 %collective-permute-start.16 = (bf16[1024,128]{1,0:T(8,128)(2,1)S(1)}, bf16[1024,128]{1,0:T(8,128)(2,1)S(1)}, u32[]{:S(2)}, u32[]{:S(2)}) collective-permute-start(bf16[1024,128]{1,0:T(8,128)(2,1)S(1)} %constant_dynamic-slice_fusion), channel_id=1, source_target_pairs={{0,1},{1,0},{2,3},{3,2},{4,5},{5,4},{6,7},{7,6},{8,9},{9,8},{10,11... | collective-permute-start | bytes 786440 | tf_op jit(solution)/shard_map/ppermute | solution.py:233
  216.9 9.2 %collective-permute-start.12 = (bf16[256,512]{1,0:T(8,128)(2,1)S(1)}, bf16[256,512]{1,0:T(8,128)(2,1)S(1)}, u32[]{:S(2)}, u32[]{:S(2)}) collective-permute-start(bf16[256,512]{1,0:T(8,128)(2,1)S(1)} %get-tuple-element.51), channel_id=1, source_target_pairs={{0,96},{4,100},{8,104},{12,108},{16,112},{20,116},{24,120},{28,124... | collective-permute-start | bytes 786440 | tf_op jit(solution)/shard_map/ppermute | solution.py:221
  218.1 15.2 %collective-permute-start.11 = (bf16[256,512]{1,0:T(8,128)(2,1)S(1)}, bf16[256,512]{1,0:T(8,128)(2,1)S(1)}, u32[]{:S(2)}, u32[]{:S(2)}) collective-permute-start(bf16[256,512]{1,0:T(8,128)(2,1)S(1)} %get-tuple-element.52), channel_id=1, source_target_pairs={{0,32},{4,36},{8,40},{12,44},{16,48},{20,52},{24,56},{28,60},{32,6... | collective-permute-start | bytes 786440 | tf_op jit(solution)/shard_map/ppermute | solution.py:221
  219.0 14.3 %collective-permute-start.10 = (bf16[256,512]{1,0:T(8,128)(2,1)S(1)}, bf16[256,512]{1,0:T(8,128)(2,1)S(1)}, u32[]{:S(2)}, u32[]{:S(2)}) collective-permute-start(bf16[256,512]{1,0:T(8,128)(2,1)S(1)} %get-tuple-element.50), channel_id=1, source_target_pairs={{0,64},{4,68},{8,72},{12,76},{16,80},{20,84},{24,88},{28,92},{32,9... | collective-permute-start | bytes 786440 | tf_op jit(solution)/shard_map/ppermute | solution.py:221
  221.7 28.5 %collective-permute-start.17 = (bf16[1024,128]{1,0:T(8,128)(2,1)S(1)}, bf16[1024,128]{1,0:T(8,128)(2,1)S(1)}, u32[]{:S(2)}, u32[]{:S(2)}) collective-permute-start(bf16[1024,128]{1,0:T(8,128)(2,1)S(1)} %add_convert_fusion.3), channel_id=1, source_target_pairs={{0,2},{1,3},{2,0},{3,1},{4,6},{5,7},{6,4},{7,5},{8,10},{9,11},{10,... | collective-permute-start | bytes 786440 | tf_op jit(solution)/shard_map/ppermute | solution.py:234
  233.5 22.9 %collective-permute-start.13 = (bf16[128,1024]{1,0:T(8,128)(2,1)S(1)}, bf16[128,1024]{1,0:T(8,128)(2,1)S(1)}, u32[]{:S(2)}, u32[]{:S(2)}) collective-permute-start(bf16[128,1024]{1,0:T(8,128)(2,1)S(1)} %fusion.49), channel_id=1, source_target_pairs={{0,4},{4,0},{8,12},{12,8},{16,20},{20,16},{24,28},{28,24},{32,36},... | collective-permute-start | bytes 786440 | tf_op jit(solution)/shard_map/ppermute | solution.py:225
  250.2 7.6 %collective-permute-start.18 = (f32[1024,128]{1,0:T(8,128)S(1)}, f32[1024,128]{1,0:T(8,128)S(1)}, u32[]{:S(2)}, u32[]{:S(2)}) collective-permute-start(f32[1024,128]{1,0:T(8,128)S(1)} %convert_add_fusion), channel_id=1, source_target_pairs={{0,1},{1,0},{2,3},{3,2},{4,5},{5,4},{6,7},{7,6},{8,9},{9,8},{10,11... | collective-permute-start | bytes 1572872 | tf_op jit(solution)/shard_map/ppermute | solution.py:235
  250.3 7.9 %copy-start.13 = (f32[2048]{0:T(1024)S(1)}, f32[2048]{0:T(1024)}, u32[]{:S(2)}) copy-start(f32[2048]{0:T(1024)} %param.17) | copy-start | bytes 24580
  250.3 8.5 %copy-start.9 = (f32[2048,128]{1,0:T(8,128)S(1)}, f32[2048,128]{1,0:T(8,128)}, u32[]{:S(2)}) copy-start(f32[2048,128]{1,0:T(8,128)} %param.16) | copy-start | bytes 3145732

commit v3 on v2

v3 whole, which is shorter than its diff:
```python
import math

import jax
import jax.numpy as jnp
from jax import lax
from jax.experimental import pallas as pl
from jax.experimental.pallas import tpu as pltpu
from jax.sharding import PartitionSpec as P

LEARN_RATE = 0.3
E = 128
N_WIDE = 32
CAP = 512
TAIL = 32
BLOCK = CAP + TAIL
N_ROWS = 2048
HI = 4
LO = N_ROWS // HI
F32 = jnp.float32
BF16 = jnp.bfloat16
LIGHT = pl.CostEstimate(flops=1, bytes_accessed=1, transcendentals=0)
APART = (2, 1, 3)


def z_perm(d):
    return [(i, ((i // 8 + d) % 4) * 8 + i % 8) for i in range(N_WIDE)]


def y_perm(d):
    return [(i, (i // 8) * 8 + (((i // 2) % 4 + d) % 4) * 2 + i % 2) for i in range(N_WIDE)]


X_LO = [(i, i ^ 1) for i in range(N_WIDE)]
CORE = [(i, i ^ 1) for i in range(4)]
X_HI = [(i, i ^ 2) for i in range(4)]


def slot_positions(onehot):
    entries, n_wide = onehot.shape
    block_len = 512
    block_count = entries // block_len
    blocked = onehot.reshape(block_count, block_len, n_wide)
    lower = (jnp.arange(block_len)[:, None] > jnp.arange(block_len)[None, :]).astype(BF16)
    within = jnp.einsum("ij,bjn->bin", lower, blocked, preferred_element_type=F32)
    block_total = jnp.sum(blocked.astype(F32), axis=1)
    before = jnp.cumsum(block_total, axis=0) - block_total
    counted = (within + before[:, None, :]) * blocked.astype(F32)
    position = jnp.sum(counted, axis=2).reshape(entries).astype(jnp.int32)
    return position, jnp.sum(block_total, axis=0).astype(jnp.int32)


def scatter_kernel(slots_ref, base_ref, far_ref, tail_ref, out_ref, rows, blocks, sems):
    dump = N_WIDE * CAP

    def clear(i, _):
        rows[pl.ds(pl.multiple_of(i * 64, 64), 64), :] = jnp.zeros((64, E), F32)
        return 0

    lax.fori_loop(0, dump // 64, clear, 0)

    def place(i, _):
        first = pl.multiple_of(i * 16, 16)
        for f in range(8):
            cols = slice(f * E, (f + 1) * E)
            tile = base_ref[pl.ds(first, 16), cols] + far_ref[pl.ds(first, 16), cols].astype(F32)
            for b in range(16):
                row = tile[b : b + 1, :]
                for j in range(2):
                    slot = slots_ref[(first + b) * 16 + 2 * f + j]
                    rows[pl.ds(slot, 1), :] = row
        return 0

    lax.fori_loop(0, base_ref.shape[0] // 16, place, 0)

    def copy_out(w):
        return pltpu.make_async_copy(blocks.at[w], out_ref.at[w], sems.at[w])

    def narrow_down(w, _):
        blocks[w, :CAP, :] = rows[pl.ds(pl.multiple_of(w * CAP, CAP), CAP), :].astype(BF16)
        blocks[w, CAP:, :] = tail_ref[w]
        copy_out(w).start()
        return 0

    lax.fori_loop(0, N_WIDE, narrow_down, 0)

    def finish(w, _):
        copy_out(w).wait()
        return 0

    lax.fori_loop(0, N_WIDE, finish, 0)


def scatter_entries(slots, base, far, tail):
    vmem = pl.BlockSpec(memory_space=pltpu.VMEM)
    return pl.pallas_call(
        scatter_kernel,
        out_shape=jax.ShapeDtypeStruct((N_WIDE, BLOCK, E), BF16),
        in_specs=[pl.BlockSpec(memory_space=pltpu.SMEM), vmem, vmem, vmem],
        out_specs=pl.BlockSpec(memory_space=pl.ANY),
        scratch_shapes=[
            pltpu.VMEM((N_WIDE * CAP + 8, E), F32),
            pltpu.VMEM((N_WIDE, BLOCK, E), BF16),
            pltpu.SemaphoreType.DMA((N_WIDE,)),
        ],
        compiler_params=pltpu.CompilerParams(vmem_limit_bytes=40 << 20),
        cost_estimate=LIGHT,
        name="place_entries",
    )(slots, base, far, tail)


def sums_kernel(count_ref, recv_ref, out_ref, bias_ref, total, left, right, todo):
    lane_rows = lax.broadcasted_iota(jnp.int32, (LO, E), 0)

    def listing(w, n):
        todo[n] = 2 * w
        n = n + jnp.where(count_ref[w] > 0, 1, 0)
        todo[n] = 2 * w + 1
        return n + jnp.where(count_ref[w] > CAP // 2, 1, 0)

    n = lax.fori_loop(0, N_WIDE, listing, 0)
    for k in range(6):
        todo[n + k] = -1
    total[...] = jnp.zeros_like(total)
    bias_ref[...] = jnp.sum(
        recv_ref[:, CAP + 8 : CAP + 16, :].astype(F32) + recv_ref[:, CAP + 16 : CAP + 24, :].astype(F32),
        axis=0,
    )

    def build(i, buf):
        for p in range(2):
            item = todo[i * 2 + p]
            w = jnp.maximum(item, 0) // 2
            half = jnp.maximum(item, 0) % 2
            ids = recv_ref[w, CAP : CAP + 16, :].astype(F32)
            row = (ids[0:4, :] * 64.0 + ids[4:8, :]).astype(jnp.int32) - 1
            row = jnp.where(half == 0, row[0:2, :], row[2:4, :])
            row = jnp.where(item < 0, -1, row)
            hi = row >> (LO.bit_length() - 1)
            lo = jnp.where(row < 0, -1, row & (LO - 1))
            hi_col = jnp.transpose(jnp.concatenate([hi] * 4, axis=0).astype(F32), (1, 0))
            for j in range(2):
                at = (2 * p + j) * E
                left[buf, :, at : at + E] = jnp.where(lane_rows == lo[j : j + 1, :], 1.0, 0.0).astype(BF16)
                v = recv_ref[w, pl.ds(pl.multiple_of(half * (CAP // 2), CAP // 2) + j * E, E), :]
                own = jnp.broadcast_to(hi_col[:, j : j + 1], (E, E)).astype(BF16)
                for h in range(HI):
                    right[buf, at : at + E, h * E : (h + 1) * E] = jnp.where(own == BF16(h), v, BF16(0))

    build(0, 0)

    def step(i, _):
        for b in range(2):
            build(2 * i + b + 1, 1 - b)
            total[...] += jnp.dot(left[b], right[b], preferred_element_type=F32)
        return 0

    lax.fori_loop(0, (n + 3) // 4, step, 0)
    for h in range(HI):
        out_ref[h * LO : (h + 1) * LO, :] = total[:, h * E : (h + 1) * E].astype(BF16)


def owned_sums(counts, recv):
    vmem = pl.BlockSpec(memory_space=pltpu.VMEM)
    return pl.pallas_call(
        sums_kernel,
        out_shape=(jax.ShapeDtypeStruct((N_ROWS, E), BF16), jax.ShapeDtypeStruct((8, E), F32)),
        in_specs=[pl.BlockSpec(memory_space=pltpu.SMEM), vmem],
        out_specs=(vmem, vmem),
        scratch_shapes=[
            pltpu.VMEM((LO, HI * E), F32),
            pltpu.VMEM((2, LO, CAP), BF16),
            pltpu.VMEM((2, CAP, HI * E), BF16),
            pltpu.SMEM((2 * N_WIDE + 16,), jnp.int32),
        ],
        compiler_params=pltpu.CompilerParams(vmem_limit_bytes=40 << 20),
        cost_estimate=LIGHT,
        name="owned_sums",
    )(counts, recv)


def summed(own, others):
    total = own.astype(F32)
    for other in others:
        total = total + other.astype(F32)
    return total


def far_kernel(block_ref, scaled_ref, embedded_ref, *refs):
    sent, turned, columns, terms, sems_in, sems_out = refs[:4], refs[4], *refs[5:]

    def copy_in(c):
        at = pl.multiple_of(block_ref[c] * 256, 256)
        return pltpu.make_async_copy(embedded_ref.at[:, pl.ds(at, 256)], columns.at[c], sems_in.at[c])

    def copy_out(q):
        return pltpu.make_async_copy(terms.at[q], sent[q], sems_out.at[q])

    for c in range(8):
        copy_in(c).start()
    turned[...] = jnp.transpose(scaled_ref[...], (1, 0))
    for route in range(2):
        part = turned[route * 512 : (route + 1) * 512, :]
        for k in range(4):
            copy_in(4 * route + k).wait()
            term = jnp.dot(part, columns[4 * route + k], preferred_element_type=F32).astype(BF16)
            for way in range(2):
                terms[2 * route + way, :, k * 256 : (k + 1) * 256] = term[way * 256 : (way + 1) * 256, :]
        for way in range(2):
            copy_out(2 * route + way).start()
    for q in range(4):
        copy_out(q).wait()


def far_terms(embedded, scaled, blocks):
    hbm = pl.BlockSpec(memory_space=pl.ANY)
    vmem = pl.BlockSpec(memory_space=pltpu.VMEM)
    return pl.pallas_call(
        far_kernel,
        out_shape=[jax.ShapeDtypeStruct((256, 1024), BF16)] * 4 + [jax.ShapeDtypeStruct((1024, 512), BF16)],
        in_specs=[pl.BlockSpec(memory_space=pltpu.SMEM), vmem, hbm],
        out_specs=[hbm] * 4 + [vmem],
        scratch_shapes=[
            pltpu.VMEM((8, 512, 256), BF16),
            pltpu.VMEM((4, 256, 1024), BF16),
            pltpu.SemaphoreType.DMA((8,)),
            pltpu.SemaphoreType.DMA((4,)),
        ],
        compiler_params=pltpu.CompilerParams(vmem_limit_bytes=40 << 20),
        cost_estimate=LIGHT,
        name="far_terms",
    )(blocks, scaled, embedded)


def near_kernel(block_ref, turned_ref, embedded_ref, *refs):
    passed, sent, columns, terms, sems_in, sems_out = refs[:4], refs[4:8], *refs[8:]

    def copy_in(c):
        at = pl.multiple_of(block_ref[c] * 256, 256)
        return pltpu.make_async_copy(embedded_ref.at[:, pl.ds(at, 256)], columns.at[c], sems_in.at[c])

    def copy_out(q):
        return pltpu.make_async_copy(terms.at[q], sent[q], sems_out.at[q])

    for c in range(16):
        copy_in(c).start()
    for q in range(4):
        route, way = q // 2, q % 2
        part = turned_ref[route * 512 : (route + 1) * 512, :]
        mine, other = slice(way * 256, (way + 1) * 256), slice((1 - way) * 256, (2 - way) * 256)
        for k in range(4):
            copy_in(4 * q + k).wait()
            at = slice(k * 256, (k + 1) * 256)
            term = jnp.dot(part, columns[4 * q + k], preferred_element_type=F32)
            terms[q, mine, at] = (term[mine, :] + passed[q][:, at].astype(F32)).astype(BF16)
            terms[q, other, at] = term[other, :].astype(BF16)
        copy_out(q).start()
    for q in range(4):
        copy_out(q).wait()


def near_terms(embedded, turned, passed, blocks):
    hbm = pl.BlockSpec(memory_space=pl.ANY)
    vmem = pl.BlockSpec(memory_space=pltpu.VMEM)
    return pl.pallas_call(
        near_kernel,
        out_shape=[jax.ShapeDtypeStruct((512, 1024), BF16)] * 4,
        in_specs=[pl.BlockSpec(memory_space=pltpu.SMEM), vmem, hbm] + [vmem] * 4,
        out_specs=[hbm] * 4,
        scratch_shapes=[
            pltpu.VMEM((16, 512, 256), BF16),
            pltpu.VMEM((4, 512, 1024), BF16),
            pltpu.SemaphoreType.DMA((16,)),
            pltpu.SemaphoreType.DMA((4,)),
        ],
        compiler_params=pltpu.CompilerParams(vmem_limit_bytes=40 << 20),
        cost_estimate=LIGHT,
        name="near_terms",
    )(blocks, turned, embedded, *passed)


def own_kernel(block_ref, turned_ref, embedded_ref, *refs):
    got, pieces, columns, sems = refs[:4], refs[4:12], *refs[12:]

    def copy_in(q):
        at = pl.multiple_of(block_ref[q] * 256, 256)
        return pltpu.make_async_copy(embedded_ref.at[:, pl.ds(at, 256)], columns.at[q], sems.at[q])

    for q in range(8):
        copy_in(q).start()
    for q in range(8):
        copy_in(q).wait()
        route = q // 4
        total = jnp.dot(
            turned_ref[route * 512 : (route + 1) * 512, :], columns[q], preferred_element_type=F32
        )
        at = pl.multiple_of(block_ref[8 + q] * 256, 256)
        for other in got[2 * route : 2 * route + 2]:
            total += other[:, pl.ds(at, 256)].astype(F32)
        pieces[q][...] = total.astype(BF16)


def own_terms(embedded, turned, got, blocks):
    hbm = pl.BlockSpec(memory_space=pl.ANY)
    vmem = pl.BlockSpec(memory_space=pltpu.VMEM)
    return pl.pallas_call(
        own_kernel,
        out_shape=[jax.ShapeDtypeStruct((512, 256), BF16)] * 8,
        in_specs=[pl.BlockSpec(memory_space=pltpu.SMEM), vmem, hbm] + [vmem] * 4,
        out_specs=[vmem] * 8,
        scratch_shapes=[pltpu.VMEM((8, 512, 256), BF16), pltpu.SemaphoreType.DMA((8,))],
        compiler_params=pltpu.CompilerParams(vmem_limit_bytes=40 << 20),
        cost_estimate=LIGHT,
        name="own_terms",
    )(blocks, turned, embedded, *got)


def weight_grad_owned(pieces, x_lo):
    got_zy = [lax.ppermute(pieces[q], "wide", y_perm(d)) for q, d in enumerate(APART)]
    got_yz = [lax.ppermute(pieces[4 + q], "wide", z_perm(d)) for q, d in enumerate(APART)]
    pair = jnp.concatenate([summed(pieces[3], got_zy), summed(pieces[7], got_yz)], axis=0).astype(BF16)
    got = lax.ppermute(lax.dynamic_slice_in_dim(pair, (1 - x_lo) * E, E, 1), "wide", X_LO)
    return summed(lax.dynamic_slice_in_dim(pair, x_lo * E, E, 1), [got]).T


def base_kernel(
    panel_ref, embedded_ref, weight_ref, bias_ref, cot_ref, scaled_ref, rows_ref, mate_ref, out_ref
):
    cross = jnp.dot(embedded_ref[...], weight_ref[...], preferred_element_type=F32) + bias_ref[...]
    backward = lax.dot_general(
        scaled_ref[...], rows_ref[...], (((1,), (1,)), ((), ())), preferred_element_type=F32
    )
    grad = cot_ref[...].astype(F32)
    out_ref[...] = grad + grad * cross + backward + mate_ref[...].astype(F32)


def base_terms(panel, embedded, weight, bias, cotangent, scaled, from_mate):
    samples, width = cotangent.shape
    tile = 256
    steps = width // tile
    return pl.pallas_call(
        base_kernel,
        out_shape=jax.ShapeDtypeStruct((samples, width), F32),
        grid_spec=pltpu.PrefetchScalarGridSpec(
            num_scalar_prefetch=1,
            grid=(steps,),
            in_specs=[
                pl.BlockSpec(embedded.shape, lambda i, p: (0, 0)),
                pl.BlockSpec((weight.shape[0], tile), lambda i, p: (0, i)),
                pl.BlockSpec((1, tile), lambda i, p: (0, i)),
                pl.BlockSpec((samples, tile), lambda i, p: (0, i)),
                pl.BlockSpec((samples, width), lambda i, p: (0, 0)),
                pl.BlockSpec((tile, width), lambda i, p: (p[0] * steps + i, 0)),
                pl.BlockSpec((samples, tile), lambda i, p: (0, i)),
            ],
            out_specs=pl.BlockSpec((samples, tile), lambda i, p: (0, i)),
        ),
        compiler_params=pltpu.CompilerParams(vmem_limit_bytes=40 << 20),
        cost_estimate=LIGHT,
        name="base_terms",
    )(panel.reshape(1), embedded, weight, bias.reshape(1, -1), cotangent, scaled, weight, from_mate)


def over_narrow(part, core):
    rows = part.shape[0] // 2
    keep = lax.dynamic_slice_in_dim(part, core * rows, rows, 0)
    send = lax.dynamic_slice_in_dim(part, (1 - core) * rows, rows, 0)
    chip = summed(keep, [lax.ppermute(send, "narrow", CORE)]).astype(BF16)
    mine = summed(chip, [lax.ppermute(chip, "narrow", X_HI)])
    mate = lax.ppermute(mine, "narrow", CORE)
    low = jnp.where(core == 0, mine, mate)
    high = jnp.where(core == 0, mate, mine)
    return jnp.concatenate([low, high], axis=0)


def body(
    embedded,
    cotangent,
    cross_weight,
    cross_bias,
    bag_size,
    row_owner,
    row_id,
    emb_table,
    adagrad_state,
):
    panel = lax.axis_index("narrow")
    wide = lax.axis_index("wide")
    z, y, x_lo = wide // 8, (wide // 2) % 4, wide % 2
    core = panel % 2
    batch_rows, width = cotangent.shape
    feats = width // E
    norm_factor = 1.0 / math.sqrt(batch_rows * N_WIDE)

    x_panel = lax.dynamic_slice_in_dim(embedded, panel * width, width, 1)
    grad_out = cotangent.astype(F32)
    scaled = (grad_out * x_panel.astype(F32)).astype(BF16)

    def backward_part(k):
        rows = lax.dynamic_slice_in_dim(cross_weight, (panel ^ k) * width, width, 0)
        return lax.dot_general(scaled, rows, (((1,), (1,)), ((), ())), preferred_element_type=F32)

    from_mate_far = lax.ppermute(backward_part(3).astype(BF16), "narrow", CORE)
    from_mate = lax.ppermute(backward_part(1).astype(BF16), "narrow", CORE)
    chip_far = (backward_part(2) + from_mate_far.astype(F32)).astype(BF16)
    chip_far, embedded, from_mate = lax.optimization_barrier((chip_far, embedded, from_mate))
    far = lax.ppermute(chip_far, "narrow", X_HI)

    far_blocks = jnp.stack([((z + 2) % 4) * 4 + k for k in range(4)] + [k * 4 + (y + 2) % 4 for k in range(4)])
    near_blocks = jnp.stack(
        [((z + d) % 4) * 4 + k for d in (1, 3) for k in range(4)]
        + [k * 4 + (y + d) % 4 for d in (1, 3) for k in range(4)]
    )
    ways = [z_perm(1), z_perm(3), y_perm(1), y_perm(3)]
    *sent, turned = far_terms(embedded, scaled, far_blocks)
    passed = [lax.ppermute(sent[q], "wide", ways[q]) for q in range(4)]
    embedded, turned = lax.optimization_barrier((embedded, turned))
    base = base_terms(panel, embedded, cross_weight, cross_bias, cotangent, scaled, from_mate)
    embedded, base, far = lax.optimization_barrier((embedded, base, far))
    sent = near_terms(embedded, turned, passed, near_blocks)
    got = [lax.ppermute(sent[q], "wide", ways[q]) for q in range(4)]
    row_owner, row_id, *_ = lax.optimization_barrier((row_owner, row_id, sent[0]))

    bag_len = lax.dynamic_slice_in_dim(bag_size, panel * feats, feats, 1)
    bag_depth = row_id.shape[2] // feats
    is_live = (jnp.arange(bag_depth, dtype=jnp.int32)[None, None, :] < bag_len[:, :, None]).reshape(-1)
    target = jnp.where(is_live, row_owner.reshape(-1), N_WIDE)
    is_target = target[:, None] == jnp.arange(N_WIDE, dtype=jnp.int32)[None, :]
    onehot = is_target.astype(BF16)
    position, counts = slot_positions(onehot)
    slots = jnp.where(is_live, target * CAP + position, N_WIDE * CAP)
    marked = row_id.reshape(-1) + 1
    halves = jnp.concatenate(
        [
            jnp.where(is_target, (marked // 64)[:, None], 0),
            jnp.where(is_target, (marked % 64)[:, None], 0),
        ],
        axis=1,
    ).astype(BF16)
    at_position = (position[:, None] == jnp.arange(CAP, dtype=jnp.int32)[None, :]).astype(BF16)
    ids = lax.dot_general(halves, at_position, (((0,), (0,)), ((), ())), preferred_element_type=F32)
    ids = ids.astype(BF16).reshape(2, N_WIDE, CAP // E, E).transpose(1, 0, 2, 3)

    bias_part = jnp.sum(scaled, axis=0, dtype=F32)
    bias_top = lax.reduce_precision(bias_part, 8, 7)
    bias_parts = jnp.stack([bias_top, bias_part - bias_top]).astype(BF16).reshape(1, 16, E)
    count_parts = jnp.stack([counts // 64, counts % 64], axis=1).astype(BF16)
    tail = jnp.concatenate(
        [
            ids.reshape(N_WIDE, 8, E),
            jnp.broadcast_to(bias_parts, (N_WIDE, 16, E)),
            jnp.broadcast_to(jnp.repeat(count_parts, 4, axis=1)[:, :, None], (N_WIDE, 8, E)),
        ],
        axis=1,
    )

    payload = scatter_entries(slots, base, far, tail)
    payload, *got = lax.optimization_barrier((payload, *got))
    recv = lax.all_to_all(payload, "wide", split_axis=0, concat_axis=0, tiled=True)
    recv_counts = (recv[:, CAP + 24, 0].astype(F32) * 64.0 + recv[:, CAP + 28, 0].astype(F32)).astype(jnp.int32)
    sums, bias_sums = owned_sums(recv_counts, recv)
    bias_grad = bias_sums.reshape(-1) * norm_factor
    row_grad = over_narrow(sums, core)
    new_state = adagrad_state + jnp.mean(row_grad * row_grad, axis=1)
    new_table = emb_table - LEARN_RATE * row_grad / jnp.sqrt(new_state)[:, None]

    later = APART + (0,)
    own_blocks = jnp.stack(
        [z * 4 + (y + d) % 4 for d in later]
        + [((z + d) % 4) * 4 + y for d in later]
        + [(y + d) % 4 for d in later]
        + [(z + d) % 4 for d in later]
    )
    weight_grad = weight_grad_owned(own_terms(embedded, turned, got, own_blocks), x_lo) * norm_factor
    return (weight_grad, bias_grad, new_table, new_state)


def solution(mesh):
    in_specs = (
        P("wide", None),
        P("wide", "narrow"),
        P(None, "narrow"),
        P("narrow"),
        P("wide", None),
        P("narrow", "wide", None, None),
        P("narrow", "wide", None),
        P("wide", None),
        P("wide"),
    )
    out_specs = (P("wide", "narrow"), P("narrow"), P("wide", None), P("wide"))
    return jax.shard_map(body, mesh=mesh, in_specs=in_specs, out_specs=out_specs, check_vma=False)
```

time: 262 us -> 204 us (0.78)
  waiting for transfers between devices: 117 us -> 56.4 us
  Pallas kernels: 40.9 us -> 64.3 us
  matrix products: 30.3 us -> 15.4 us
  starting transfers between devices: 50.2 us -> 35.6 us
  local copies, waits for them, and re-layouts: 8.82 us -> 18.3 us
    ppermute x13 -> x15, waiting for transfers between devices: 98.4 us -> 15.3 us  [the longest x3 9.89 us: weight_grad_owned(): lax.ppermute(pieces[4 + q], 'wide', z_perm(d))]
    all_to_all x1, waiting for transfers between devices: 0.01 us -> 41.1 us  [body(): lax.all_to_all(payload, 'wide', split_axis=0, concat_axis=0, tiled=True)]
    pallas_call x1 -> x4, Pallas kernels: 10.8 us -> 30.2 us  [the longest x1 10.3 us: near_terms(): pl.pallas_call(near_kernel, out_shape=[jax.ShapeDtypeStruct((512, 1024),...]
    ppermute x1, waiting for transfers between devices: 19 us -> 0.01 us  [body(): far = lax.ppermute(chip_far, 'narrow', X_HI)]
    dot_general x3 -> x0, matrix products: 11.7 us -> none  [the longest x1 5.85 us: body(): jnp.dot(embedded, cross_weight, preferred_element_type=F32) + cross_bias]
    ppermute x13 -> x15, starting transfers between devices: 34.2 us -> 23.3 us  [the longest x1 6.27 us: weight_grad_owned(): lax.ppermute(lax.dynamic_slice_in_dim(pair, (1 - x_lo) * E, E, 1), 'wide'...]
    unnamed x36 -> x34, local copies, waits for them, and re-layouts: 2.3 us -> 13.1 us
    pallas_call x1, Pallas kernels: 12.4 us -> 18.9 us  [scatter_entries(): pl.pallas_call(scatter_kernel, out_shape=jax.ShapeDtypeStruct((N_WIDE, BL...]
  transfers between devices with their start and end apart: 20 -> 22, of which waited for: 6 -> 4; matrix products, arithmetic and copies ran while one was open for 13% -> 13% of each run, Pallas kernels for 7% -> 27%
where the time goes in v3:
time: 204 us
  Pallas kernels  64.3 us (32%)
  waiting for transfers between devices  56.4 us (28%)
  starting transfers between devices  35.6 us (17%)
  local copies, waits for them, and re-layouts  18.3 us (9%)
  matrix products  15.4 us (8%)
  other arithmetic  12.5 us (6%)
    all_to_all x1, waiting for transfers between devices, body(): lax.all_to_all(payload, 'wide', split_axis=0, concat_axis=0, tiled=True)  41.1 us
    pallas_call x1, Pallas kernels, scatter_entries(): pl.pallas_call(scatter_kernel, out_shape=jax.ShapeDtypeStruct((N_WIDE, BL...  18.9 us
    pallas_call x1, Pallas kernels, owned_sums(): pl.pallas_call(sums_kernel, out_shape=(jax.ShapeDtypeStruct((N_ROWS, E),...  15.1 us
    unnamed x34, local copies, waits for them, and re-layouts  13.1 us
    dot_general x3, matrix products, backward_part(): lax.dot_general(scaled, rows, (((1,), (1,)), ((), ())), preferred_element...  10.8 us
    pallas_call x1, Pallas kernels, near_terms(): pl.pallas_call(near_kernel, out_shape=[jax.ShapeDtypeStruct((512, 1024),...  10.3 us
    ppermute x3, waiting for transfers between devices, weight_grad_owned(): lax.ppermute(pieces[4 + q], 'wide', z_perm(d))  9.89 us
    pallas_call x1, Pallas kernels, base_terms(): pl.pallas_call(base_kernel, out_shape=jax.ShapeDtypeStruct((samples, widt...  8.27 us
  transfers between devices with their start and end apart: 22, of which 4 were waited for; matrix products, arithmetic and copies ran while one was open for 13% of the time, Pallas kernels for 27%

profile of v3, /device:TPU:24, one launch (start us, length us, event | category | flops | bytes accessed | tf_op | source)
XLA Modules:
  0.0 203.7 jit_solution(14714773142429419141)
XLA Ops:
  0.7 2.0 convert_reduce_fusion
  2.7 2.9 %fusion.8 = bf16[512,1024]{1,0:T(8,128)(2,1)S(1)} fusion(bf16[512,1024]{1,0:T(8,128)(2,1)S(1)} %get-tuple-element.93.scaled_ref, bf16[4096,1024]{1,0:T(8,128)(2,1)} %rows_ref.1, s32[]{:T(128)S(6)} %select_n.235), kind=kOutput, calls=%fused_computation.16 | convolution fusion | flops 1074266112 | bytes 4194308 | tf_op jit(solution)/shard_map/dot_general | solution.py:400
  5.7 3.9 %fusion.11 = bf16[512,1024]{1,0:T(8,128)(2,1)} fusion(bf16[512,1024]{1,0:T(8,128)(2,1)S(1)} %get-tuple-element.93.scaled_ref, bf16[4096,1024]{1,0:T(8,128)(2,1)} %rows_ref.1, s32[]{:T(128)S(6)} %select_n.236), kind=kOutput, calls=%fused_computation.17 | convolution fusion | flops 1074266112 | bytes 4194308 | tf_op jit(solution)/shard_map/dot_general | solution.py:400
  10.0 4.1 %add_convert_fusion = bf16[512,1024]{1,0:T(8,128)(2,1)} fusion(bf16[512,1024]{1,0:T(8,128)(2,1)} %collective-permute-done, bf16[512,1024]{1,0:T(8,128)(2,1)S(1)} %get-tuple-element.93.scaled_ref, bf16[4096,1024]{1,0:T(8,128)(2,1)} %rows_ref.1, s32[]{:T(128)S(6)} %select_n.234), kind=kOutput, calls=%fused_computation.7 | convolution fusion | flops 1075314688 | bytes 5242884 | tf_op jit(solution)/shard_map/dot_general | solution.py:400
  14.1 3.0 %collective-permute-start.2 = (bf16[512,1024]{1,0:T(8,128)(2,1)}, bf16[512,1024]{1,0:T(8,128)(2,1)}, u32[]{:S(2)}, u32[]{:S(2)}) collective-permute-start(bf16[512,1024]{1,0:T(8,128)(2,1)} %add_convert_fusion), channel_id=1, source_target_pairs={{0,2},{1,3},{2,0},{3,1},{4,6},{5,7},{6,4},{7,5},{8,10},{9,11},{10,... | collective-permute-start | bytes 3145736 | tf_op jit(solution)/shard_map/ppermute | solution.py:406
  17.4 2.2 %copy-done.1 = bf16[512,4096]{1,0:T(8,128)(2,1)S(1)} copy-done((bf16[512,4096]{1,0:T(8,128)(2,1)S(1)}, bf16[512,4096]{1,0:T(8,128)(2,1)}, u32[]{:S(2)}) %copy-start.1) | copy-done | bytes 4194328
  19.6 5.7 %far_terms.1 = (bf16[256,1024]{1,0:T(8,128)(2,1)}, bf16[256,1024]{1,0:T(8,128)(2,1)}, bf16[256,1024]{1,0:T(8,128)(2,1)}, bf16[256,1024]{1,0:T(8,128)(2,1)}, bf16[1024,512]{1,0:T(8,128)(2,1)S(1)}) custom-call(s32[8]{0:T(128)S(1)} %stack.159.block_ref, bf16[512,1024]{1,0:T(8,128)(2,1)S(1)} %get-tuple-element.93.scaled_ref, bf16[512,4096]{1,0:T(8,128)(2,1)S(1)} %copy-done.1), custom_call_target="tpu_custom_call" | custom-call | flops 1 | bytes 1 | tf_op jit(solution)/shard_map/far_terms/pallas_call | solution.py:217
  25.3 1.0 copy-done.6
  26.3 1.9 collective-permute-start.3
  28.2 2.1 %collective-permute-start.4 = (bf16[256,1024]{1,0:T(8,128)(2,1)}, bf16[256,1024]{1,0:T(8,128)(2,1)}, u32[]{:S(2)}, u32[]{:S(2)}) collective-permute-start(bf16[256,1024]{1,0:T(8,128)(2,1)} %get-tuple-element.46), channel_id=1, source_target_pairs={{0,96},{4,100},{8,104},{12,108},{16,112},{20,116},{24,120},{28,124... | collective-permute-start | bytes 1572872 | tf_op jit(solution)/shard_map/ppermute | solution.py:415
  30.5 1.8 collective-permute-start.6
  32.3 1.3 iota_compare_fusion.2
  33.7 1.6 lt.191
  35.2 1.6 lt.192
  37.0 2.2 %copy-done.2 = bf16[512,4096]{1,0:T(8,128)(2,1)S(1)} copy-done((bf16[512,4096]{1,0:T(8,128)(2,1)S(1)}, bf16[512,4096]{1,0:T(8,128)(2,1)}, u32[]{:S(2)}) %copy-start.2) | copy-done | bytes 4194328
  39.2 1.2 copy-done.5
  40.4 1.2 copy-done.10
  41.6 8.3 %base_terms.1.base_ref = f32[512,1024]{1,0:T(8,128)S(1)} custom-call(s32[1]{0:T(128)} %bitcast.23.panel_ref, bf16[512,4096]{1,0:T(8,128)(2,1)S(1)} %copy-done.2, bf16[4096,1024]{1,0:T(8,128)(2,1)} %rows_ref.1, f32[1,1024]{1,0:T(1,128)S(1)} %bitcast.88, bf16[512,1024]{1,0:T(8,128)(2,1)S(1)} %copy-done.5, bf16[512,1024]{1,0:T(8,128)(2,1)S(1)} %get-tuple-element.93.scaled_ref, ...), custom_call_target="tpu_custom_call" | custom-call | flops 1 | bytes 1 | tf_op jit(solution)/shard_map/base_terms/pallas_call | solution.py:340
  50.0 10.3 %near_terms.1 = (bf16[512,1024]{1,0:T(8,128)(2,1)}, bf16[512,1024]{1,0:T(8,128)(2,1)}, bf16[512,1024]{1,0:T(8,128)(2,1)}, bf16[512,1024]{1,0:T(8,128)(2,1)}) custom-call(s32[16]{0:T(128)S(1)} %stack.174.block_ref, bf16[1024,512]{1,0:T(8,128)(2,1)S(1)} %copy-done.7, bf16[512,4096]{1,0:T(8,128)(2,1)S(1)} %copy-done.2, ...), custom_call_target="tpu_custom_call" | custom-call | flops 1 | bytes 1 | tf_op jit(solution)/shard_map/near_terms/pallas_call | solution.py:264
  62.1 3.3 %collective-permute-start.8 = (bf16[512,1024]{1,0:T(8,128)(2,1)}, bf16[512,1024]{1,0:T(8,128)(2,1)}, u32[]{:S(2)}, u32[]{:S(2)}) collective-permute-start(bf16[512,1024]{1,0:T(8,128)(2,1)} %get-tuple-element.54), channel_id=1, source_target_pairs={{0,96},{4,100},{8,104},{12,108},{16,112},{20,116},{24,120},{28,124... | collective-permute-start | bytes 3145736 | tf_op jit(solution)/shard_map/ppermute | solution.py:420
  65.3 1.4 collective-permute-start.9
  66.8 0.6 collective-permute-start.10
  67.4 0.9 select_convert_fusion.1
  68.5 3.9 %fusion.18 = bf16[64,512]{1,0:T(8,128)(2,1)S(1)} fusion(s32[8192]{0:T(1024)S(1)} %bitcast.91, bf16[8192,32]{0,1:T(8,128)(2,1)} %get-tuple-element.99, bf16[8192,32]{0,1:T(8,128)(2,1)S(1)} %get-tuple-element.98), kind=kOutput, calls=%fused_computation.21 | convolution fusion | flops 543195136 | bytes 1146880 | tf_op jit(solution)/shard_map/dot_general | solution.py:440
  72.6 18.9 %place_entries.1 = bf16[32,544,128]{2,1,0:T(8,128)(2,1)S(1)} custom-call(s32[8192]{0:T(1024)S(1)} %get-tuple-element.106.slots_ref, f32[512,1024]{1,0:T(8,128)S(1)} %base_terms.1.base_ref, bf16[512,1024]{1,0:T(8,128)(2,1)} %collective-permute-done.2.far_ref, bf16[32,32,128]{2,1,0:T(8,128)(2,1)S(1)} %pad_maximum_fusion.1.tail_ref), custom_call_target="tpu_custom_call" | custom-call | flops 1 | bytes 1 | tf_op jit(solution)/shard_map/place_entries/pallas_call | solution.py:95
  91.6 2.0 copy-done.4
  93.6 7.3 %all-to-all-start = ((bf16[32,544,128]{2,1,0:T(8,128)(2,1)}), bf16[32,544,128]{2,1,0:T(8,128)(2,1)}, u32[]{:S(2)}, u32[]{:S(2)}) async-start(bf16[32,544,128]{2,1,0:T(8,128)(2,1)} %copy-done.4), calls=%async_computation | async-start | bytes 8912896 | tf_op jit(solution)/shard_map/all_to_all | solution.py:458
  101.1 2.2 %copy-done.3 = bf16[512,4096]{1,0:T(8,128)(2,1)S(1)} copy-done((bf16[512,4096]{1,0:T(8,128)(2,1)S(1)}, bf16[512,4096]{1,0:T(8,128)(2,1)}, u32[]{:S(2)}) %copy-start.3) | copy-done | bytes 4194328
  103.3 6.0 %own_terms.1 = (bf16[512,256]{1,0:T(8,128)(2,1)S(1)}, bf16[512,256]{1,0:T(8,128)(2,1)S(1)}, bf16[512,256]{1,0:T(8,128)(2,1)S(1)}, bf16[512,256]{1,0:T(8,128)(2,1...) custom-call(s32[16]{0:T(128)S(1)} %stack.151.block_ref, ...), custom_call_target="tpu_custom_call" | custom-call | flops 1 | bytes 1 | tf_op jit(solution)/shard_map/own_terms/pallas_call | solution.py:305
  109.3 0.9 collective-permute-start.13
  110.2 2.4 %collective-permute-start.12 = (bf16[512,256]{1,0:T(8,128)(2,1)S(1)}, bf16[512,256]{1,0:T(8,128)(2,1)S(1)}, u32[]{:S(2)}, u32[]{:S(2)}) collective-permute-start(bf16[512,256]{1,0:T(8,128)(2,1)S(1)} %get-tuple-element.63), channel_id=1, source_target_pairs={{0,8},{4,12},{8,16},{12,20},{16,24},{20,28},{24,0},{28,4},{32,40},... | collective-permute-start | bytes 786440 | tf_op jit(solution)/shard_map/ppermute | solution.py:318
  112.8 41.1 %all-to-all-done.recv_ref = bf16[32,544,128]{2,1,0:T(8,128)(2,1)} async-done(((bf16[32,544,128]{2,1,0:T(8,128)(2,1)}), bf16[32,544,128]{2,1,0:T(8,128)(2,1)}, u32[]{:S(2)}, u32[]{:S(2)}) %all-to-all-start) | async-done | bytes 4456480 | tf_op jit(solution)/shard_map/all_to_all | solution.py:458
  153.9 1.6 fusion.33.count_ref
  155.5 15.1 %owned_sums.1 = (bf16[2048,128]{1,0:T(8,128)(2,1)S(1)}, f32[8,128]{1,0:T(8,128)S(1)}) custom-call(s32[32]{0:T(128)S(1)} %fusion.33.count_ref, bf16[32,544,128]{2,1,0:T(8,128)(2,1)} %all-to-all-done.recv_ref), custom_call_target="tpu_custom_call" | custom-call | flops 1 | bytes 1 | tf_op jit(solution)/shard_map/owned_sums/pallas_call | solution.py:164
  170.6 0.7 constant_dynamic-slice_fusion
  171.4 2.0 collective-permute-start.15
  173.4 1.1 add_convert_fusion.3
  174.5 1.0 add_convert_fusion.1
  175.5 1.5 collective-permute-start.19
  177.0 3.4 %collective-permute-done.16 = bf16[512,256]{1,0:T(8,128)(2,1)S(1)} collective-permute-done((bf16[512,256]{1,0:T(8,128)(2,1)S(1)}, bf16[512,256]{1,0:T(8,128)(2,1)S(1)}, u32[]{:S(2)}, u32[]{:S(2)}) %collective-permute-start.16) | collective-permute-done | bytes 262176 | tf_op jit(solution)/shard_map/ppermute | solution.py:319
  180.5 6.5 %collective-permute-done.15 = bf16[512,256]{1,0:T(8,128)(2,1)S(1)} collective-permute-done((bf16[512,256]{1,0:T(8,128)(2,1)S(1)}, bf16[512,256]{1,0:T(8,128)(2,1)S(1)}, u32[]{:S(2)}, u32[]{:S(2)}) %collective-permute-start.15) | collective-permute-done | bytes 262176 | tf_op jit(solution)/shard_map/ppermute | solution.py:319
  187.1 6.3 %collective-permute-start.17 = (bf16[1024,128]{1,0:T(8,128)(2,1)S(1)}, bf16[1024,128]{1,0:T(8,128)(2,1)S(1)}, u32[]{:S(2)}, u32[]{:S(2)}) collective-permute-start(bf16[1024,128]{1,0:T(8,128)(2,1)S(1)} %fusion.26), channel_id=1, source_target_pairs={{0,4},{4,0},{8,12},{12,8},{16,20},{20,16},{24,28},{28,24},{32,36},... | collective-permute-start | bytes 786440 | tf_op jit(solution)/shard_map/ppermute | solution.py:321
  193.4 0.8 convert_add_fusion
  194.2 5.3 %collective-permute-done.17 = bf16[1024,128]{1,0:T(8,128)(2,1)S(1)} collective-permute-done((bf16[1024,128]{1,0:T(8,128)(2,1)S(1)}, bf16[1024,128]{1,0:T(8,128)(2,1)S(1)}, u32[]{:S(2)}, u32[]{:S(2)}) %collective-permute-start.17) | collective-permute-done | bytes 262176 | tf_op jit(solution)/shard_map/ppermute | solution.py:321
  199.7 1.0 copy.37
  200.7 0.6 multiply_bitcast_fusion.1
  201.7 0.6 fusion.41
  202.3 1.3 divide_subtract_fusion
  (88 shorter events, 4.3 us)
Async XLA Ops:
  0.6 16.5 %copy-start = (s32[512,32]{0,1:T(8,128)S(1)}, s32[512,32]{0,1:T(8,128)}, u32[]{:S(2)}) copy-start(s32[512,32]{0,1:T(8,128)} %param.13) | copy-start | bytes 196612
  5.6 4.4 %collective-permute-start = (bf16[512,1024]{1,0:T(8,128)(2,1)S(1)}, bf16[512,1024]{1,0:T(8,128)(2,1)}, u32[]{:S(2)}, u32[]{:S(2)}) collective-permute-start(bf16[512,1024]{1,0:T(8,128)(2,1)S(1)} %fusion.8), channel_id=1, source_target_pairs={{0,1},{1,0},{2,3},{3,2},{4,5},{5,4},{6,7},{7,6},{8,9},{9,8},{10,11... | collective-permute-start | bytes 3145736 | tf_op jit(solution)/shard_map/ppermute | solution.py:402
  9.5 4.6 %collective-permute-start.1 = (bf16[512,1024]{1,0:T(8,128)(2,1)}, bf16[512,1024]{1,0:T(8,128)(2,1)S(1)}, u32[]{:S(2)}, u32[]{:S(2)}) collective-permute-start(bf16[512,1024]{1,0:T(8,128)(2,1)} %fusion.11), channel_id=1, source_target_pairs={{0,1},{1,0},{2,3},{3,2},{4,5},{5,4},{6,7},{7,6},{8,9},{9,8},{10,11... | collective-permute-start | bytes 3145736 | tf_op jit(solution)/shard_map/ppermute | solution.py:403
  14.1 11.2 %copy-start.9 = (bf16[512,1024]{1,0:T(8,128)(2,1)}, bf16[512,1024]{1,0:T(8,128)(2,1)S(1)}, u32[]{:S(2)}) copy-start(bf16[512,1024]{1,0:T(8,128)(2,1)S(1)} %collective-permute-done.1.mate_ref) | copy-start | bytes 3145732
  14.1 35.8 %collective-permute-start.2 = (bf16[512,1024]{1,0:T(8,128)(2,1)}, bf16[512,1024]{1,0:T(8,128)(2,1)}, u32[]{:S(2)}, u32[]{:S(2)}) collective-permute-start(bf16[512,1024]{1,0:T(8,128)(2,1)} %add_convert_fusion), channel_id=1, source_target_pairs={{0,2},{1,3},{2,0},{3,1},{4,6},{5,7},{6,4},{7,5},{8,10},{9,11},{10,... | collective-permute-start | bytes 3145736 | tf_op jit(solution)/shard_map/ppermute | solution.py:406
  17.4 2.2 %copy-start.1 = (bf16[512,4096]{1,0:T(8,128)(2,1)S(1)}, bf16[512,4096]{1,0:T(8,128)(2,1)}, u32[]{:S(2)}) copy-start(bf16[512,4096]{1,0:T(8,128)(2,1)} %embedded_ref.3) | copy-start | bytes 12582916
  19.6 17.4 %copy-start.11 = (f32[1024]{0:T(1024)S(1)}, f32[1024]{0:T(1024)}, u32[]{:S(2)}) copy-start(f32[1024]{0:T(1024)} %param.12) | copy-start | bytes 12292
  25.3 1.0 copy-start.6
  26.3 23.7 %collective-permute-start.3 = (bf16[256,1024]{1,0:T(8,128)(2,1)}, bf16[256,1024]{1,0:T(8,128)(2,1)}, u32[]{:S(2)}, u32[]{:S(2)}) collective-permute-start(bf16[256,1024]{1,0:T(8,128)(2,1)} %get-tuple-element.45), channel_id=1, source_target_pairs={{0,32},{4,36},{8,40},{12,44},{16,48},{20,52},{24,56},{28,60},{32,6... | collective-permute-start | bytes 1572872 | tf_op jit(solution)/shard_map/ppermute | solution.py:415
  28.2 21.7 %collective-permute-start.4 = (bf16[256,1024]{1,0:T(8,128)(2,1)}, bf16[256,1024]{1,0:T(8,128)(2,1)}, u32[]{:S(2)}, u32[]{:S(2)}) collective-permute-start(bf16[256,1024]{1,0:T(8,128)(2,1)} %get-tuple-element.46), channel_id=1, source_target_pairs={{0,96},{4,100},{8,104},{12,108},{16,112},{20,116},{24,120},{28,124... | collective-permute-start | bytes 1572872 | tf_op jit(solution)/shard_map/ppermute | solution.py:415
  30.3 19.6 %collective-permute-start.5 = (bf16[256,1024]{1,0:T(8,128)(2,1)}, bf16[256,1024]{1,0:T(8,128)(2,1)}, u32[]{:S(2)}, u32[]{:S(2)}) collective-permute-start(bf16[256,1024]{1,0:T(8,128)(2,1)} %get-tuple-element.47), channel_id=1, source_target_pairs={{0,8},{4,12},{8,16},{12,20},{16,24},{20,28},{24,0},{28,4},{32,40},... | collective-permute-start | bytes 1572872 | tf_op jit(solution)/shard_map/ppermute | solution.py:415
  30.5 19.4 %collective-permute-start.6 = (bf16[256,1024]{1,0:T(8,128)(2,1)}, bf16[256,1024]{1,0:T(8,128)(2,1)}, u32[]{:S(2)}, u32[]{:S(2)}) collective-permute-start(bf16[256,1024]{1,0:T(8,128)(2,1)} %get-tuple-element.48), channel_id=1, source_target_pairs={{0,24},{4,28},{8,0},{12,4},{16,8},{20,12},{24,16},{28,20},{32,56},... | collective-permute-start | bytes 1572872 | tf_op jit(solution)/shard_map/ppermute | solution.py:415
  37.0 2.2 %copy-start.2 = (bf16[512,4096]{1,0:T(8,128)(2,1)S(1)}, bf16[512,4096]{1,0:T(8,128)(2,1)}, u32[]{:S(2)}) copy-start(bf16[512,4096]{1,0:T(8,128)(2,1)} %embedded_ref.3) | copy-start | bytes 12582916
  39.2 1.2 copy-start.5
  40.4 1.2 copy-start.10
  41.6 8.4 %copy-start.7 = (bf16[1024,512]{1,0:T(8,128)(2,1)S(1)}, bf16[1024,512]{1,0:T(8,128)(2,1)}, u32[]{:S(2)}) copy-start(bf16[1024,512]{1,0:T(8,128)(2,1)} %copy-done.6) | copy-start | bytes 3145732
  49.9 10.4 %copy-start.13 = (s32[1,512,16,1]{1,3,2,0:T(1,128)S(1)}, s32[1,512,16,1]{1,3,2,0:T(1,128)}, u32[]{:S(2)}) copy-start(s32[1,512,16,1]{1,3,2,0:T(1,128)} %param.14) | copy-start | bytes 98308
  49.9 10.9 %copy-start.14 = (s32[1,512,16]{1,2,0:T(8,128)S(1)}, s32[1,512,16]{1,2,0:T(8,128)}, u32[]{:S(2)}) copy-start(s32[1,512,16]{1,2,0:T(8,128)} %param.15) | copy-start | bytes 98308
  60.7 32.9 %collective-permute-start.7 = (bf16[512,1024]{1,0:T(8,128)(2,1)}, bf16[512,1024]{1,0:T(8,128)(2,1)}, u32[]{:S(2)}, u32[]{:S(2)}) collective-permute-start(bf16[512,1024]{1,0:T(8,128)(2,1)} %get-tuple-element.49), channel_id=1, source_target_pairs={{0,32},{4,36},{8,40},{12,44},{16,48},{20,52},{24,56},{28,60},{32,6... | collective-permute-start | bytes 3145736 | tf_op jit(solution)/shard_map/ppermute | solution.py:420
  62.1 31.6 %collective-permute-start.8 = (bf16[512,1024]{1,0:T(8,128)(2,1)}, bf16[512,1024]{1,0:T(8,128)(2,1)}, u32[]{:S(2)}, u32[]{:S(2)}) collective-permute-start(bf16[512,1024]{1,0:T(8,128)(2,1)} %get-tuple-element.54), channel_id=1, source_target_pairs={{0,96},{4,100},{8,104},{12,108},{16,112},{20,116},{24,120},{28,124... | collective-permute-start | bytes 3145736 | tf_op jit(solution)/shard_map/ppermute | solution.py:420
  65.3 28.3 %collective-permute-start.9 = (bf16[512,1024]{1,0:T(8,128)(2,1)}, bf16[512,1024]{1,0:T(8,128)(2,1)}, u32[]{:S(2)}, u32[]{:S(2)}) collective-permute-start(bf16[512,1024]{1,0:T(8,128)(2,1)} %get-tuple-element.55), channel_id=1, source_target_pairs={{0,8},{4,12},{8,16},{12,20},{16,24},{20,28},{24,0},{28,4},{32,40},... | collective-permute-start | bytes 3145736 | tf_op jit(solution)/shard_map/ppermute | solution.py:420
  66.8 26.9 %collective-permute-start.10 = (bf16[512,1024]{1,0:T(8,128)(2,1)}, bf16[512,1024]{1,0:T(8,128)(2,1)}, u32[]{:S(2)}, u32[]{:S(2)}) collective-permute-start(bf16[512,1024]{1,0:T(8,128)(2,1)} %get-tuple-element.56), channel_id=1, source_target_pairs={{0,24},{4,28},{8,0},{12,4},{16,8},{20,12},{24,16},{28,20},{32,56},... | collective-permute-start | bytes 3145736 | tf_op jit(solution)/shard_map/ppermute | solution.py:420
  91.6 2.0 %copy-start.4 = (bf16[32,544,128]{2,1,0:T(8,128)(2,1)}, bf16[32,544,128]{2,1,0:T(8,128)(2,1)S(1)}, u32[]{:S(2)}) copy-start(bf16[32,544,128]{2,1,0:T(8,128)(2,1)S(1)} %place_entries.1) | copy-start | bytes 13369348
  93.6 7.5 %copy-start.8 = (bf16[1024,512]{1,0:T(8,128)(2,1)S(1)}, bf16[1024,512]{1,0:T(8,128)(2,1)}, u32[]{:S(2)}) copy-start(bf16[1024,512]{1,0:T(8,128)(2,1)} %copy-done.6) | copy-start | bytes 3145732
  93.6 60.2 %all-to-all-start = ((bf16[32,544,128]{2,1,0:T(8,128)(2,1)}), bf16[32,544,128]{2,1,0:T(8,128)(2,1)}, u32[]{:S(2)}, u32[]{:S(2)}) async-start(bf16[32,544,128]{2,1,0:T(8,128)(2,1)} %copy-done.4), calls=%async_computation | async-start | bytes 8912896 | tf_op jit(solution)/shard_map/all_to_all | solution.py:458
  101.1 2.2 %copy-start.3 = (bf16[512,4096]{1,0:T(8,128)(2,1)S(1)}, bf16[512,4096]{1,0:T(8,128)(2,1)}, u32[]{:S(2)}) copy-start(bf16[512,4096]{1,0:T(8,128)(2,1)} %embedded_ref.3) | copy-start | bytes 12582916
  109.3 62.1 %collective-permute-start.13 = (bf16[512,256]{1,0:T(8,128)(2,1)S(1)}, bf16[512,256]{1,0:T(8,128)(2,1)S(1)}, u32[]{:S(2)}, u32[]{:S(2)}) collective-permute-start(bf16[512,256]{1,0:T(8,128)(2,1)S(1)} %get-tuple-element.64), channel_id=1, source_target_pairs={{0,24},{4,28},{8,0},{12,4},{16,8},{20,12},{24,16},{28,20},{32,56},... | collective-permute-start | bytes 786440 | tf_op jit(solution)/shard_map/ppermute | solution.py:318
  110.2 63.2 %collective-permute-start.12 = (bf16[512,256]{1,0:T(8,128)(2,1)S(1)}, bf16[512,256]{1,0:T(8,128)(2,1)S(1)}, u32[]{:S(2)}, u32[]{:S(2)}) collective-permute-start(bf16[512,256]{1,0:T(8,128)(2,1)S(1)} %get-tuple-element.63), channel_id=1, source_target_pairs={{0,8},{4,12},{8,16},{12,20},{16,24},{20,28},{24,0},{28,4},{32,40},... | collective-permute-start | bytes 786440 | tf_op jit(solution)/shard_map/ppermute | solution.py:318
  112.6 60.8 %collective-permute-start.11 = (bf16[512,256]{1,0:T(8,128)(2,1)S(1)}, bf16[512,256]{1,0:T(8,128)(2,1)}, u32[]{:S(2)}, u32[]{:S(2)}) collective-permute-start(bf16[512,256]{1,0:T(8,128)(2,1)S(1)} %get-tuple-element.62), channel_id=1, source_target_pairs={{0,16},{4,20},{8,24},{12,28},{16,0},{20,4},{24,8},{28,12},{32,48},... | collective-permute-start | bytes 786440 | tf_op jit(solution)/shard_map/ppermute | solution.py:318
  171.3 3.2 %collective-permute-start.18 = (bf16[1024,128]{1,0:T(8,128)(2,1)}, bf16[1024,128]{1,0:T(8,128)(2,1)}, u32[]{:S(2)}, u32[]{:S(2)}) collective-permute-start(bf16[1024,128]{1,0:T(8,128)(2,1)} %constant_dynamic-slice_fusion), channel_id=1, source_target_pairs={{0,1},{1,0},{2,3},{3,2},{4,5},{5,4},{6,7},{7,6},{8,9},{9,8},{10,11... | collective-permute-start | bytes 786440 | tf_op jit(solution)/shard_map/ppermute | solution.py:367
  171.3 9.1 %collective-permute-start.16 = (bf16[512,256]{1,0:T(8,128)(2,1)S(1)}, bf16[512,256]{1,0:T(8,128)(2,1)S(1)}, u32[]{:S(2)}, u32[]{:S(2)}) collective-permute-start(bf16[512,256]{1,0:T(8,128)(2,1)S(1)} %get-tuple-element.68), channel_id=1, source_target_pairs={{0,96},{4,100},{8,104},{12,108},{16,112},{20,116},{24,120},{28,124... | collective-permute-start | bytes 786440 | tf_op jit(solution)/shard_map/ppermute | solution.py:319
  171.4 15.5 %collective-permute-start.15 = (bf16[512,256]{1,0:T(8,128)(2,1)S(1)}, bf16[512,256]{1,0:T(8,128)(2,1)S(1)}, u32[]{:S(2)}, u32[]{:S(2)}) collective-permute-start(bf16[512,256]{1,0:T(8,128)(2,1)S(1)} %get-tuple-element.67), channel_id=1, source_target_pairs={{0,32},{4,36},{8,40},{12,44},{16,48},{20,52},{24,56},{28,60},{32,6... | collective-permute-start | bytes 786440 | tf_op jit(solution)/shard_map/ppermute | solution.py:319
  173.4 13.5 %collective-permute-start.14 = (bf16[512,256]{1,0:T(8,128)(2,1)S(1)}, bf16[512,256]{1,0:T(8,128)(2,1)S(1)}, u32[]{:S(2)}, u32[]{:S(2)}) collective-permute-start(bf16[512,256]{1,0:T(8,128)(2,1)S(1)} %get-tuple-element.66), channel_id=1, source_target_pairs={{0,64},{4,68},{8,72},{12,76},{16,80},{20,84},{24,88},{28,92},{32,9... | collective-permute-start | bytes 786440 | tf_op jit(solution)/shard_map/ppermute | solution.py:319
  175.5 17.8 %collective-permute-start.19 = (bf16[1024,128]{1,0:T(8,128)(2,1)S(1)}, bf16[1024,128]{1,0:T(8,128)(2,1)S(1)}, u32[]{:S(2)}, u32[]{:S(2)}) collective-permute-start(bf16[1024,128]{1,0:T(8,128)(2,1)S(1)} %add_convert_fusion.1), channel_id=1, source_target_pairs={{0,2},{1,3},{2,0},{3,1},{4,6},{5,7},{6,4},{7,5},{8,10},{9,11},{10,... | collective-permute-start | bytes 786440 | tf_op jit(solution)/shard_map/ppermute | solution.py:368
  187.1 12.5 %collective-permute-start.17 = (bf16[1024,128]{1,0:T(8,128)(2,1)S(1)}, bf16[1024,128]{1,0:T(8,128)(2,1)S(1)}, u32[]{:S(2)}, u32[]{:S(2)}) collective-permute-start(bf16[1024,128]{1,0:T(8,128)(2,1)S(1)} %fusion.26), channel_id=1, source_target_pairs={{0,4},{4,0},{8,12},{12,8},{16,20},{20,16},{24,28},{28,24},{32,36},... | collective-permute-start | bytes 786440 | tf_op jit(solution)/shard_map/ppermute | solution.py:321
  194.2 7.0 %collective-permute-start.20 = (f32[1024,128]{1,0:T(8,128)}, f32[1024,128]{1,0:T(8,128)S(1)}, u32[]{:S(2)}, u32[]{:S(2)}) collective-permute-start(f32[1024,128]{1,0:T(8,128)} %convert_add_fusion), channel_id=1, source_target_pairs={{0,1},{1,0},{2,3},{3,2},{4,5},{5,4},{6,7},{7,6},{8,9},{9,8},{10,11... | collective-permute-start | bytes 1572872 | tf_op jit(solution)/shard_map/ppermute | solution.py:369
  199.6 2.1 %copy-start.15 = (f32[2048]{0:T(1024)S(1)}, f32[2048]{0:T(1024)}, u32[]{:S(2)}) copy-start(f32[2048]{0:T(1024)} %param.17) | copy-start | bytes 24580
  199.6 2.7 %copy-start.12 = (f32[2048,128]{1,0:T(8,128)S(1)}, f32[2048,128]{1,0:T(8,128)}, u32[]{:S(2)}) copy-start(f32[2048,128]{1,0:T(8,128)} %param.16) | copy-start | bytes 3145732
